TPU v7x, 32 devices: a whole 2x2x4 slice. The times are simulated.
32 devices in a mesh: span: 8 (over z, core), wall: 4 (over y, x).
Axes of the slice: x: 2, y: 2, z: 4, core: 2. Of those that a mesh axis runs over, the one named last changes fastest.
Arguments:
- field: float32 [5, 5, 5, 8, 8, 128], P(None, None, None, 'span', 'wall'), may hold values from -6 to 6
- velocity: float32 [3, 5, 5, 5, 8, 8, 128], P(None, None, None, None, 'span', 'wall'), may hold values from -6 to 6
- cells: int32 [4096], P(('span', 'wall')), may hold values from 0 to 255
- destination: int32 [4096, 1], P(('span', 'wall')), may hold values from 0 to 7; in each aligned block of 128 rows (0 to 127, 128 to 255, ...) at most 16 rows name the same one
- targets: bfloat16 [4096, 128], P(('span', 'wall')), may hold values from -6 to 6
- weight_in: bfloat16 [8, 128, 256], P('span'), may hold values from -0.5 to 0.5
- weight_two: bfloat16 [8, 256, 256], P('span'), may hold values from -0.375 to 0.375
- weight_three: bfloat16 [8, 256, 256], P('span'), may hold values from -0.375 to 0.375
- weight_four: bfloat16 [8, 256, 256], P('span'), may hold values from -0.375 to 0.375
- weight_out: bfloat16 [8, 256, 128], P('span'), may hold values from -0.375 to 0.375
Outputs:
- new_field: float32 [5, 5, 5, 8, 8, 128], P(None, None, None, 'span', 'wall')
- grad_in: float32 [8, 128, 256], P('span')
- grad_two: float32 [8, 256, 256], P('span')
- grad_three: float32 [8, 256, 256], P('span')
- grad_four: float32 [8, 256, 256], P('span')
- grad_out: float32 [8, 256, 128], P('span')
Inputs may be any that keep to these rules, and one draw needn't show every extreme that they name: `cells`: A local element index of the owning device. `destination`: among the 128 rows of one device at most 16 name the same station, and in every draw some device has exactly 16 rows naming one station.
All inputs are finite; a program needn't handle non-finite values.
Results may differ from a plain program's by a relative error of at most 0.0065.
Values may be sent and summed in bfloat16 or wider, within the bound.
A program may use at most 64 MiB of HBM per device.

v0:
```python
import math

import jax
import jax.numpy as jnp
from jax import lax
from jax.sharding import PartitionSpec as P

P_SIZE = 5
S = 128
FEAT = 128


step_scale = 0.04


def extended(x, sides, width):
    for axis, dim in sides:
        size, length = (lax.axis_size(axis), x.shape[dim])
        up = [(i, (i + 1) % size) for i in range(size - 1)]
        down = [(j, i) for i, j in up]
        last = lax.slice_in_dim(x, length - width, length, axis=dim)
        first = lax.slice_in_dim(x, 0, width, axis=dim)
        before = lax.ppermute(last, axis, up)
        after = lax.ppermute(first, axis, down)
        x = jnp.concatenate([before, x, after], axis=dim)
    return x


def legendre_pair(order, point):
    value_prev = 1.0
    value_now = point
    slope_prev = 0.0
    slope_now = 1.0
    for degree in range(1, order):
        value_next = ((2 * degree + 1) * point * value_now - degree * value_prev) / (degree + 1)
        slope_next = slope_prev + (2 * degree + 1) * value_now
        value_prev, value_now = (value_now, value_next)
        slope_prev, slope_now = (slope_now, slope_next)
    return (value_now, slope_now)


def gauss_nodes(count):
    found = []
    for index in range(count):
        guess = math.cos(math.pi * (index + 0.75) / (count + 0.5))
        for sweep in range(60):
            value, slope = legendre_pair(count, guess)
            guess = guess - value / slope
        found.append(guess)
    return sorted(found)


def fr_tables():
    nodes = gauss_nodes(P_SIZE)
    bary = []
    for j in range(P_SIZE):
        product = 1.0
        for m in range(P_SIZE):
            if m != j:
                product = product * (nodes[j] - nodes[m])
        bary.append(1.0 / product)
    deriv = [[0.0] * P_SIZE for row_index in range(P_SIZE)]
    for i in range(P_SIZE):
        for j in range(P_SIZE):
            if i != j:
                deriv[i][j] = bary[j] / bary[i] / (nodes[i] - nodes[j])
        deriv[i][i] = -sum((deriv[i][j] for j in range(P_SIZE) if j != i))

    def basis_at(point):
        values = []
        for j in range(P_SIZE):
            product = 1.0
            for m in range(P_SIZE):
                if m != j:
                    product = product * (point - nodes[m]) / (nodes[j] - nodes[m])
            values.append(product)
        return values

    left_value = basis_at(-1.0)
    right_value = basis_at(1.0)
    sign = (-1.0) ** P_SIZE
    slope_left = [
        0.5 * sign * (legendre_pair(P_SIZE, x)[1] - legendre_pair(P_SIZE - 1, x)[1]) for x in nodes
    ]
    slope_right = [-slope_left[P_SIZE - 1 - i] for i in range(P_SIZE)]
    return tuple(
        (
            jnp.asarray(table, jnp.float32)
            for table in (deriv, left_value, right_value, slope_left, slope_right)
        )
    )


def along(matrix, field, axis):
    return jnp.moveaxis(
        jnp.tensordot(matrix, field, axes=([1], [axis]), precision=lax.Precision.HIGHEST), 0, axis
    )


def at_face(vector, field, axis):
    return jnp.tensordot(vector, field, axes=([0], [axis]), precision=lax.Precision.HIGHEST)


def spread(face, vector, axis, ndim):
    target_shape = [1] * ndim
    target_shape[axis] = vector.shape[0]
    return jnp.expand_dims(face, axis) * vector.reshape(target_shape)


def upwind(state_before, speed_before, state_after, speed_after):
    mean_speed = 0.5 * (speed_before + speed_after)
    return 0.5 * mean_speed * (state_before + state_after) - 0.5 * jnp.abs(mean_speed) * (
        state_after - state_before
    )


def face_states(field, speed, axis, tables):
    left_value = tables[1]
    right_value = tables[2]
    return (
        at_face(left_value, field, axis),
        at_face(left_value, speed, axis),
        at_face(right_value, field, axis),
        at_face(right_value, speed, axis),
    )


def divergence(field, speed, axis, own, before, after, tables):
    deriv, left_value, right_value, slope_left, slope_right = tables
    flux = speed * field
    volume = along(deriv, flux, axis)
    flux_left = at_face(left_value, flux, axis)
    flux_right = at_face(right_value, flux, axis)
    common_left = upwind(before[0], before[1], own[0], own[1])
    common_right = upwind(own[2], own[3], after[0], after[1])
    return (
        volume
        + spread(common_left - flux_left, slope_left, axis, field.ndim)
        + spread(common_right - flux_right, slope_right, axis, field.ndim)
    )


def forward(inputs, weights):
    acts = [inputs]
    pres = []
    hidden = inputs
    for layer in weights[:-1]:
        pre = jnp.dot(hidden, layer, preferred_element_type=jnp.float32)
        pres.append(pre)
        hidden = jax.nn.silu(pre).astype(jnp.bfloat16)
        acts.append(hidden)
    return (jnp.dot(hidden, weights[-1], preferred_element_type=jnp.float32), acts, pres)


def backward_layer(error, weight, pre):
    back = lax.dot_general(
        error, weight, (((1,), (1,)), ((), ())), preferred_element_type=jnp.float32
    )
    sigma = jax.nn.sigmoid(pre)
    return (back * sigma * (1.0 + pre * (1.0 - sigma))).astype(jnp.bfloat16)


def weight_grad(act, error):
    return lax.dot_general(act, error, (((0,), (0,)), ((), ())), preferred_element_type=jnp.float32)


def neighbour_faces(direction, field, own):
    count = field.shape[3 + direction]
    face_axis = 3 + direction
    stacked = jnp.stack(own)
    if direction == 0:
        padded = extended(stacked, (("span", 3),), 1)
    else:
        padded = extended(stacked, (("wall", 4),), 1)
    before = lax.slice_in_dim(padded[2:4], 0, count, axis=face_axis)
    after = lax.slice_in_dim(padded[0:2], 2, count + 2, axis=face_axis)
    return ((before[0], before[1]), (after[0], after[1]))


def local(
    field,
    velocity,
    cells,
    destination,
    targets,
    weight_in,
    weight_two,
    weight_three,
    weight_four,
    weight_out,
):
    tables = fr_tables()
    total = jnp.zeros_like(field)
    for direction in range(3):
        speed = velocity[direction]
        own = face_states(field, speed, direction, tables)
        if direction < 2:
            before, after = neighbour_faces(direction, field, own)
        else:
            before = (jnp.roll(own[2], 1, 4), jnp.roll(own[3], 1, 4))
            after = (jnp.roll(own[0], -1, 4), jnp.roll(own[1], -1, 4))
        total = total + divergence(field, speed, direction, own, before, after, tables)
    new_field = field - step_scale * total
    local_count = field.shape[3] * field.shape[4] * field.shape[5]
    speed_means = jnp.mean(velocity.reshape(3, P_SIZE * P_SIZE * P_SIZE, local_count), axis=1)
    values = jnp.concatenate(
        [new_field.reshape(P_SIZE * P_SIZE * P_SIZE, local_count), speed_means], axis=0
    )
    rows = jnp.take(values, cells, axis=1).T.astype(jnp.bfloat16)
    span_count = lax.axis_size("span")
    slot_count = S // 8
    dest = destination[:, 0]
    onehot = (dest[:, None] == jnp.arange(span_count, dtype=jnp.int32)[None, :]).astype(jnp.int32)
    slots = jnp.sum((jnp.cumsum(onehot, axis=0) - 1) * onehot, axis=1)
    position = dest * slot_count + slots
    row_buffer = jnp.zeros((span_count * slot_count, FEAT), jnp.bfloat16).at[position].set(rows)
    target_buffer = (
        jnp.zeros((span_count * slot_count, targets.shape[1]), jnp.bfloat16)
        .at[position]
        .set(targets)
    )
    flag_buffer = (
        jnp.zeros((span_count * slot_count,), jnp.bfloat16)
        .at[position]
        .set(jnp.ones((rows.shape[0],), jnp.bfloat16))
    )
    got_rows, got_targets, got_flags = (
        lax.all_to_all(
            row_buffer.reshape(span_count, slot_count, FEAT),
            "span",
            split_axis=0,
            concat_axis=0,
            tiled=True,
        ),
        lax.all_to_all(
            target_buffer.reshape(span_count, slot_count, -1),
            "span",
            split_axis=0,
            concat_axis=0,
            tiled=True,
        ),
        lax.all_to_all(
            flag_buffer.reshape(span_count, slot_count),
            "span",
            split_axis=0,
            concat_axis=0,
            tiled=True,
        ),
    )
    inputs = got_rows.reshape(span_count * slot_count, FEAT)
    wanted = got_targets.reshape(span_count * slot_count, -1).astype(jnp.float32)
    flags = got_flags.reshape(span_count * slot_count).astype(jnp.float32)
    row_scale = flags / jnp.maximum(jnp.sum(flags), 1.0)
    layer_one = weight_in[0]
    layer_two = weight_two[0]
    layer_three = weight_three[0]
    layer_four = weight_four[0]
    layer_last = weight_out[0]
    weights = (layer_one, layer_two, layer_three, layer_four, layer_last)
    output, acts, pres = forward(inputs, weights)
    error = (row_scale[:, None] * (output - wanted)).astype(jnp.bfloat16)
    grad_last = weight_grad(acts[4], error)
    error = backward_layer(error, layer_last, pres[3])
    grad_fourth = weight_grad(acts[3], error)
    error = backward_layer(error, layer_four, pres[2])
    grad_third = weight_grad(acts[2], error)
    error = backward_layer(error, layer_three, pres[1])
    grad_second = weight_grad(acts[1], error)
    error = backward_layer(error, layer_two, pres[0])
    grad_first = weight_grad(acts[0], error)
    grad_first, grad_second, grad_third, grad_fourth, grad_last = lax.psum(
        (grad_first, grad_second, grad_third, grad_fourth, grad_last), "wall"
    )
    return (
        new_field,
        grad_first[None],
        grad_second[None],
        grad_third[None],
        grad_fourth[None],
        grad_last[None],
    )


def solution(mesh):
    in_specs = (
        P(None, None, None, "span", "wall", None),
        P(None, None, None, None, "span", "wall", None),
        P(("span", "wall")),
        P(("span", "wall"), None),
        P(("span", "wall"), None),
        P("span", None, None),
        P("span", None, None),
        P("span", None, None),
        P("span", None, None),
        P("span", None, None),
    )
    out_specs = (
        P(None, None, None, "span", "wall", None),
        P("span", None, None),
        P("span", None, None),
        P("span", None, None),
        P("span", None, None),
        P("span", None, None),
    )
    return jax.shard_map(local, mesh=mesh, in_specs=in_specs, out_specs=out_specs, check_vma=False)
```

profile of v0, /device:TPU:0, one launch (start us, length us, event | category | flops | bytes accessed | tf_op | source)
XLA Modules:
  0.0 135.0 jit_solution(14415722476873485441)
XLA Ops:
  7.2 0.7 copy-done.8
  7.9 1.2 fusion.53
  9.4 1.1 slice_bitcast_fusion.2
  11.3 1.3 collective-permute-start.1
  12.6 3.0 %collective-permute-start = (f32[4,5,5,1,2,128]{5,0,4,3,2,1:T(4,128)S(1)}, f32[4,5,5,1,2,128]{5,0,4,3,2,1:T(4,128)S(1)}, u32[]{:S(2)}, u32[]{:S(2)}) collective-permute-start(f32[4,5,5,1,2,128]{5,0,4,3,2,1:T(4,128)S(1)} %pad_maximum_fusion.1), channel_id=1, source_target_pairs={{0,4},{4,8},{8,12},{12,16},{16,20},{20,24},{24,28},{1,5},{5,9},{9,... | collective-permute-start | bytes 307208 | tf_op jit(solution)/shard_map/ppermute | solution.py:23
  16.1 1.3 scatter_custom_fusion.1
  17.4 0.7 all_to_all.16
  18.1 6.3 %all-to-all-start.1 = ((bf16[8,1,16]{2,1,0:T(2,128)(2,1)}), bf16[8,1,16]{2,1,0:T(2,128)(2,1)S(1)}, u32[]{:S(2)}, u32[]{:S(2)}) async-start(bf16[8,1,16]{2,1,0:T(2,128)(2,1)} %all_to_all.16), calls=%async_computation.1 | async-start | bytes 8192 | tf_op jit(solution)/shard_map/all_to_all | solution.py:242
  25.8 3.6 %collective-permute-start.2 = (f32[4,5,5,1,1,128]{5,0,4,3,2,1:T(4,128)S(1)}, f32[4,5,5,1,1,128]{5,0,4,3,2,1:T(4,128)S(1)}, u32[]{:S(2)}, u32[]{:S(2)}) collective-permute-start(f32[4,5,5,1,1,128]{5,0,4,3,2,1:T(4,128)S(1)} %get-tuple-element.43), channel_id=1, source_target_pairs={{0,1},{1,2},{2,3},{4,5},{5,6},{6,7},{8,9},{9,10},{10,11},{12,13},{... | collective-permute-start | bytes 153608 | tf_op jit(solution)/shard_map/ppermute | solution.py:23
  29.4 1.3 collective-permute-start.3
  37.0 1.7 %scatter_custom_fusion.2 = bf16[128,128]{1,0:T(8,128)(2,1)} fusion(s32[128]{0:T(128)S(1)} %fusion.87, bf16[128,128]{1,0:T(8,128)(2,1)} %param.19, bf16[]{:T(256)} %constant.56.clone.1), kind=kCustom, calls=%fused_computation.144 | custom fusion | bytes 33280 | tf_op jit(solution)/shard_map/scatter | solution.py:220
  38.9 0.6 convert_reduce_fusion
  40.8 0.6 copy-done.11
  42.1 1.7 %scatter_custom_fusion = bf16[128,128]{1,0:T(8,128)(2,1)} fusion(s32[128]{0:T(128)S(1)} %fusion.87, f32[]{:T(128)} %constant.65.clone.1, pred[128]{0:T(512)(128)(4,1)S(1)} %compare_and_fusion, bf16[]{:T(256)} %constant.56.clone.1, f32[128,256]{0,1:T(8,128)S(1)} %pad_maximum_fusion, s32[1024]{0:T(1024)S(1)} %pad_clamp_fusion), kind=kCustom, calls=%fused_computation.117 | custom fusion | flops 16384 | bytes 168454 | tf_op jit(solution)/shard_map/scatter | solution.py:216
  43.9 5.2 %all-to-all-start = ((bf16[8,16,128]{2,1,0:T(8,128)(2,1)}), bf16[8,16,128]{2,1,0:T(8,128)(2,1)S(1)}, u32[]{:S(2)}, u32[]{:S(2)}) async-start(bf16[8,16,128]{2,1,0:T(8,128)(2,1)} %bitcast.133), calls=%async_computation | async-start | bytes 65536 | tf_op jit(solution)/shard_map/all_to_all | solution.py:228
  49.2 5.6 %all-to-all-done = bf16[8,16,128]{2,1,0:T(8,128)(2,1)S(1)} async-done(((bf16[8,16,128]{2,1,0:T(8,128)(2,1)}), bf16[8,16,128]{2,1,0:T(8,128)(2,1)S(1)}, u32[]{:S(2)}, u32[]{:S(2)}) %all-to-all-start) | async-done | bytes 32800 | tf_op jit(solution)/shard_map/all_to_all | solution.py:228
  54.8 3.3 %all-to-all-start.2 = ((bf16[8,16,128]{2,1,0:T(8,128)(2,1)}), bf16[8,16,128]{2,1,0:T(8,128)(2,1)S(1)}, u32[]{:S(2)}, u32[]{:S(2)}) async-start(bf16[8,16,128]{2,1,0:T(8,128)(2,1)} %bitcast.140), calls=%async_computation.2 | async-start | bytes 65536 | tf_op jit(solution)/shard_map/all_to_all | solution.py:235
  58.4 0.7 copy-done.15
  59.3 0.7 copy-done.14
  60.3 3.5 %all-to-all-done.2 = bf16[8,16,128]{2,1,0:T(8,128)(2,1)S(1)} async-done(((bf16[8,16,128]{2,1,0:T(8,128)(2,1)}), bf16[8,16,128]{2,1,0:T(8,128)(2,1)S(1)}, u32[]{:S(2)}, u32[]{:S(2)}) %all-to-all-start.2) | async-done | bytes 32800 | tf_op jit(solution)/shard_map/all_to_all | solution.py:235
  64.2 0.9 convolution_bitcast_fusion.3
  65.5 1.0 convolution_bitcast_fusion.1
  66.5 0.9 convolution_bitcast_fusion
  67.4 1.0 convolution_bitcast_fusion.4
  68.4 0.9 convolution_bitcast_fusion.2
  69.4 0.7 copy.95
  70.1 52.7 %all-reduce.3.cloned.1.call-done = (f32[1,128,256]{2,1,0:T(8,128)}, f32[1,256,256]{2,1,0:T(8,128)}, f32[1,256,256]{2,1,0:T(8,128)}, f32[1,256,256]{2,1,0:T(8,128)}, f32[1,256,128]{2,1,0:T(8,128)}) async-done(((f32[1,128,256]{2,1,0:T(8,128)}, f32[1,256,256]{2,1,0:T(8,128)}, f32[1,256,256]{2,1,0:T(8,128)}, f32[1,256,256]{2,1,0:T(8,128)}, f32[1,256,128]{2,1,0:T(8,128)}), (f32[1,128,256]{2,1,0:T(8,128)}, ...) | async-done | bytes 1048592 | tf_op jit(solution)/shard_map/psum | solution.py:271
  122.8 1.6 %copy.197 = f32[1,128,256]{2,1,0:T(8,128)} copy(f32[1,128,256]{2,1,0:T(8,128)} %get-tuple-element.50) | data formatting | bytes 262144
  124.4 0.7 copy.198
  125.4 0.7 copy.199
  126.5 0.7 copy.200
  127.5 0.7 copy.201
  (115 shorter events, 12.9 us)
Async XLA Ops:
  7.2 53.0 %copy-start = (bf16[1,256,256]{2,1,0:T(8,128)(2,1)S(1)}, bf16[1,256,256]{2,1,0:T(8,128)(2,1)}, u32[]{:S(2)}) copy-start(bf16[1,256,256]{2,1,0:T(8,128)(2,1)} %param.23) | copy-start | bytes 393220
  7.2 0.7 copy-start.8
  7.2 1.9 %copy-start.1 = (f32[5,5,5,1,2,128]{5,4,3,2,1,0:T(2,128)S(1)}, f32[5,5,5,1,2,128]{5,4,3,2,1,0:T(2,128)}, u32[]{:S(2)}) copy-start(f32[5,5,5,1,2,128]{5,4,3,2,1,0:T(2,128)} %param.15) | copy-start | bytes 384004
  7.9 1.2 copy-start.9
  11.2 4.4 %copy-start.13 = (s32[128,1]{0,1:T(1,128)S(1)}, s32[128,1]{0,1:T(1,128)}, u32[]{:S(2)}) copy-start(s32[128,1]{0,1:T(1,128)} %param.18) | copy-start | bytes 1540
  11.3 29.2 %collective-permute-start.1 = (f32[4,5,5,1,2,128]{5,0,4,3,2,1:T(4,128)S(1)}, f32[4,5,5,1,2,128]{5,0,4,3,2,1:T(4,128)S(1)}, u32[]{:S(2)}, u32[]{:S(2)}) collective-permute-start(f32[4,5,5,1,2,128]{5,0,4,3,2,1:T(4,128)S(1)} %pad_maximum_fusion.1), channel_id=1, source_target_pairs={{4,0},{8,4},{12,8},{16,12},{20,16},{24,20},{28,24},{5,1},{9,5},{13... | collective-permute-start | bytes 307208 | tf_op jit(solution)/shard_map/ppermute | solution.py:24
  12.6 28.1 %collective-permute-start = (f32[4,5,5,1,2,128]{5,0,4,3,2,1:T(4,128)S(1)}, f32[4,5,5,1,2,128]{5,0,4,3,2,1:T(4,128)S(1)}, u32[]{:S(2)}, u32[]{:S(2)}) collective-permute-start(f32[4,5,5,1,2,128]{5,0,4,3,2,1:T(4,128)S(1)} %pad_maximum_fusion.1), channel_id=1, source_target_pairs={{0,4},{4,8},{8,12},{12,16},{16,20},{20,24},{24,28},{1,5},{5,9},{9,... | collective-permute-start | bytes 307208 | tf_op jit(solution)/shard_map/ppermute | solution.py:23
  18.1 20.7 %all-to-all-start.1 = ((bf16[8,1,16]{2,1,0:T(2,128)(2,1)}), bf16[8,1,16]{2,1,0:T(2,128)(2,1)S(1)}, u32[]{:S(2)}, u32[]{:S(2)}) async-start(bf16[8,1,16]{2,1,0:T(2,128)(2,1)} %all_to_all.16), calls=%async_computation.1 | async-start | bytes 8192 | tf_op jit(solution)/shard_map/all_to_all | solution.py:242
  25.7 5.0 %copy-start.17 = (s32[128]{0:T(128)S(1)}, s32[128]{0:T(128)}, u32[]{:S(2)}) copy-start(s32[128]{0:T(128)} %param.17) | copy-start | bytes 1540
  25.8 5.6 %copy-start.2 = (f32[3,5,5,5,1,2,128]{6,5,4,3,2,1,0:T(2,128)S(1)}, f32[3,5,5,5,1,2,128]{6,5,4,3,2,1,0:T(2,128)}, u32[]{:S(2)}) copy-start(f32[3,5,5,5,1,2,128]{6,5,4,3,2,1,0:T(2,128)} %param.16) | copy-start | bytes 1152004
  25.8 14.3 %collective-permute-start.2 = (f32[4,5,5,1,1,128]{5,0,4,3,2,1:T(4,128)S(1)}, f32[4,5,5,1,1,128]{5,0,4,3,2,1:T(4,128)S(1)}, u32[]{:S(2)}, u32[]{:S(2)}) collective-permute-start(f32[4,5,5,1,1,128]{5,0,4,3,2,1:T(4,128)S(1)} %get-tuple-element.43), channel_id=1, source_target_pairs={{0,1},{1,2},{2,3},{4,5},{5,6},{6,7},{8,9},{9,10},{10,11},{12,13},{... | collective-permute-start | bytes 153608 | tf_op jit(solution)/shard_map/ppermute | solution.py:23
  29.4 10.9 %collective-permute-start.3 = (f32[4,5,5,1,1,128]{5,0,4,3,2,1:T(4,128)S(1)}, f32[4,5,5,1,1,128]{5,0,4,3,2,1:T(4,128)S(1)}, u32[]{:S(2)}, u32[]{:S(2)}) collective-permute-start(f32[4,5,5,1,1,128]{5,0,4,3,2,1:T(4,128)S(1)} %get-tuple-element.44), channel_id=1, source_target_pairs={{1,0},{2,1},{3,2},{5,4},{6,5},{7,6},{9,8},{10,9},{11,10},{13,12},{... | collective-permute-start | bytes 153608 | tf_op jit(solution)/shard_map/ppermute | solution.py:24
  33.1 0.7 copy-start.10
  40.7 0.7 copy-start.11
  40.7 0.7 copy-start.12
  43.9 14.4 %copy-start.7 = (bf16[1,128,256]{2,1,0:T(8,128)(2,1)S(1)}, bf16[1,128,256]{2,1,0:T(8,128)(2,1)}, u32[]{:S(2)}) copy-start(bf16[1,128,256]{2,1,0:T(8,128)(2,1)} %param.20) | copy-start | bytes 196612
  43.9 11.0 %all-to-all-start = ((bf16[8,16,128]{2,1,0:T(8,128)(2,1)}), bf16[8,16,128]{2,1,0:T(8,128)(2,1)S(1)}, u32[]{:S(2)}, u32[]{:S(2)}) async-start(bf16[8,16,128]{2,1,0:T(8,128)(2,1)} %bitcast.133), calls=%async_computation | async-start | bytes 65536 | tf_op jit(solution)/shard_map/all_to_all | solution.py:228
  54.8 9.0 %all-to-all-start.2 = ((bf16[8,16,128]{2,1,0:T(8,128)(2,1)}), bf16[8,16,128]{2,1,0:T(8,128)(2,1)S(1)}, u32[]{:S(2)}, u32[]{:S(2)}) async-start(bf16[8,16,128]{2,1,0:T(8,128)(2,1)} %bitcast.140), calls=%async_computation.2 | async-start | bytes 65536 | tf_op jit(solution)/shard_map/all_to_all | solution.py:235
  58.2 0.9 copy-start.15
  58.2 64.6 %all-reduce.3.cloned.1.call-start = ((), (), s32[]{:S(2)}) async-start(), calls=%async_computation.3 | async-start | bytes 2097152 | tf_op jit(solution)/shard_map/psum | solution.py:271
  59.1 0.9 copy-start.14
  60.2 3.7 %copy-start.16 = (bf16[1,256,128]{2,1,0:T(8,128)(2,1)S(1)}, bf16[1,256,128]{2,1,0:T(8,128)(2,1)}, u32[]{:S(2)}) copy-start(bf16[1,256,128]{2,1,0:T(8,128)(2,1)} %param.24) | copy-start | bytes 196612
  122.8 1.6 %copy-start.5 = (f32[1,256,256]{2,1,0:T(8,128)S(1)}, f32[1,256,256]{2,1,0:T(8,128)}, u32[]{:S(2)}) copy-start(f32[1,256,256]{2,1,0:T(8,128)} %get-tuple-element.51) | copy-start | bytes 786436
  124.4 1.0 copy-start.4
  125.4 1.0 copy-start.3
  126.5 1.0 copy-start.6
Sparse Core Ops, SparseCore 0:
  69.5 53.2 all-reduce.2
where the time goes:
time: 136 us; the launch traced here: 135 us
  waiting for transfers between devices  61.8 us (45%)
  starting transfers between devices  24.1 us (18%)
  local copies, waits for them, and re-layouts  16 us (12%)
  between operations  15.4 us (11%)
  matrix products  13.6 us (10%)
  other arithmetic  4.08 us (3%)
    psum x1, waiting for transfers between devices, local(): lax.psum((grad_first, grad_second, grad_third, grad_fourth, grad_last), '...  52.7 us
    unnamed x44, local copies, waits for them, and re-layouts  9.25 us
    ppermute x2, starting transfers between devices, extended(): before = lax.ppermute(last, axis, up)  6.6 us
    dot_general x18, matrix products, at_face(): jnp.tensordot(vector, field, axes=([0], [axis]), precision=lax.Precision....  6.38 us
    all_to_all x1, starting transfers between devices, local(): lax.all_to_all(flag_buffer.reshape(span_count, slot_count), 'span', split...  6.31 us
    all_to_all x1, waiting for transfers between devices, local(): lax.all_to_all(row_buffer.reshape(span_count, slot_count, FEAT), 'span',...  5.64 us
    all_to_all x1, starting transfers between devices, local(): lax.all_to_all(row_buffer.reshape(span_count, slot_count, FEAT), 'span',...  5.21 us
    dot_general x5, matrix products, weight_grad(): lax.dot_general(act, error, (((0,), (0,)), ((), ())), preferred_element_t...  4.75 us
  transfers between devices with their start and end apart: 8, of which 3 were waited for; matrix products, arithmetic and copies ran while one was open for 10% of the time, Pallas kernels for 0%

commit v1 on v0

v1 whole, which is shorter than its diff:
```python
import functools
import math

import jax
import jax.numpy as jnp
import numpy as np
from jax import lax
from jax.experimental import pallas as pl
from jax.experimental.pallas import tpu as pltpu
from jax.sharding import PartitionSpec as P

P_SIZE = 5
CAP = 16
MESH = pl.DeviceIdType.MESH


step_scale = 0.04


def legendre_pair(order, point):
    value_prev = 1.0
    value_now = point
    slope_prev = 0.0
    slope_now = 1.0
    for degree in range(1, order):
        value_next = ((2 * degree + 1) * point * value_now - degree * value_prev) / (degree + 1)
        slope_next = slope_prev + (2 * degree + 1) * value_now
        value_prev, value_now = (value_now, value_next)
        slope_prev, slope_now = (slope_now, slope_next)
    return (value_now, slope_now)


def gauss_nodes(count):
    found = []
    for index in range(count):
        guess = math.cos(math.pi * (index + 0.75) / (count + 0.5))
        for sweep in range(60):
            value, slope = legendre_pair(count, guess)
            guess = guess - value / slope
        found.append(guess)
    return sorted(found)


def fr_tables():
    nodes = gauss_nodes(P_SIZE)
    bary = []
    for j in range(P_SIZE):
        product = 1.0
        for m in range(P_SIZE):
            if m != j:
                product = product * (nodes[j] - nodes[m])
        bary.append(1.0 / product)
    deriv = [[0.0] * P_SIZE for row_index in range(P_SIZE)]
    for i in range(P_SIZE):
        for j in range(P_SIZE):
            if i != j:
                deriv[i][j] = bary[j] / bary[i] / (nodes[i] - nodes[j])
        deriv[i][i] = -sum((deriv[i][j] for j in range(P_SIZE) if j != i))

    def basis_at(point):
        values = []
        for j in range(P_SIZE):
            product = 1.0
            for m in range(P_SIZE):
                if m != j:
                    product = product * (point - nodes[m]) / (nodes[j] - nodes[m])
            values.append(product)
        return values

    left_value = basis_at(-1.0)
    right_value = basis_at(1.0)
    sign = (-1.0) ** P_SIZE
    slope_left = [
        0.5 * sign * (legendre_pair(P_SIZE, x)[1] - legendre_pair(P_SIZE - 1, x)[1]) for x in nodes
    ]
    slope_right = [-slope_left[P_SIZE - 1 - i] for i in range(P_SIZE)]
    inner = [
        [
            step_scale
            * (deriv[i][m] - slope_left[i] * left_value[m] - slope_right[i] * right_value[m])
            for m in range(P_SIZE)
        ]
        for i in range(P_SIZE)
    ]
    edge_left = [0.25 * step_scale * s for s in slope_left]
    edge_right = [0.25 * step_scale * s for s in slope_right]
    return inner, left_value, right_value, edge_left, edge_right


INNER, LEFT, RIGHT, EDGE_LEFT, EDGE_RIGHT = fr_tables()
RANGE = range(P_SIZE)


def weighted(table, parts):
    total = parts[0] * np.float32(table[0])
    for weight, part in zip(table[1:], parts[1:]):
        total = total + part * np.float32(weight)
    return total


def upwind(state_before, speed_before, state_after, speed_after):
    speed = speed_before + speed_after
    return speed * (state_before + state_after) - jnp.abs(speed) * (state_after - state_before)


def swap(x):
    return jnp.concatenate([x[..., 1:2, :], x[..., 0:1, :]], axis=-2)


def shift(x, step):
    return jnp.concatenate([x[..., -step:], x[..., :-step]], axis=-1)


def section_kernel(
    spans, walls,
    field_hbm, velocity_hbm, cells_ref, dest_ref, targets_ref,
    new_ref, rows_all, marks_all,
    field, velocity, own_zero, own_one, zero_before, zero_after, one_before, one_after,
    flat, rows_send, marks_send,
    in_sems, halo_send, halo_recv,
    marks_a_send, marks_a_recv, marks_b_send, marks_b_recv,
    rows_a_send, rows_a_recv, rows_b_send, rows_b_recv,
):
    i = lax.axis_index("span")
    w = lax.axis_index("wall")
    loads = [pltpu.make_async_copy(field_hbm, field, in_sems.at[0])]
    for d in range(3):
        loads.append(pltpu.make_async_copy(velocity_hbm.at[d], velocity.at[d], in_sems.at[1 + d]))
    for load in loads:
        load.start()

    barrier = pltpu.get_barrier_semaphore()
    for d in range(1, spans):
        pl.semaphore_signal(barrier, inc=1, device_id={"span": lax.rem(i + d, spans)}, device_id_type=MESH)
    for d in range(1, walls):
        pl.semaphore_signal(barrier, inc=1, device_id={"wall": lax.rem(w + d, walls)}, device_id_type=MESH)

    for at_end, ref in ((i == 0, zero_before), (i == spans - 1, zero_after), (w == 0, one_before), (w == walls - 1, one_after)):
        @pl.when(at_end)
        def _(ref=ref):
            ref[...] = jnp.zeros_like(ref)

    loads[0].wait()
    loads[1].wait()
    for j in RANGE:
        q = [field[m, j] for m in RANGE]
        a = [velocity[0, m, j] for m in RANGE]
        own_zero[0, j] = weighted(LEFT, q)
        own_zero[1, j] = weighted(LEFT, a)
        own_zero[2, j] = weighted(RIGHT, q)
        own_zero[3, j] = weighted(RIGHT, a)
    loads[2].wait()
    for m0 in RANGE:
        q = [field[m0, m] for m in RANGE]
        a = [velocity[1, m0, m] for m in RANGE]
        own_one[0, m0] = weighted(LEFT, q)
        own_one[1, m0] = weighted(LEFT, a)
        own_one[2, m0] = weighted(RIGHT, q)
        own_one[3, m0] = weighted(RIGHT, a)

    pl.semaphore_wait(barrier, spans + walls - 2)

    def halo(number, axis, place, count, own, into, right):
        peer = jnp.minimum(place + 1, count - 1) if right else jnp.maximum(place - 1, 0)
        copy = pltpu.make_async_remote_copy(
            src_ref=own.at[pl.ds(2 if right else 0, 2)],
            dst_ref=into,
            send_sem=halo_send.at[number],
            recv_sem=halo_recv.at[number],
            device_id={axis: peer},
            device_id_type=MESH,
        )
        sends = place < count - 1 if right else place > 0
        gets = place > 0 if right else place < count - 1
        return copy, sends, gets

    halos = [
        halo(0, "span", i, spans, own_zero, zero_before, True),
        halo(1, "span", i, spans, own_zero, zero_after, False),
        halo(2, "wall", w, walls, own_one, one_before, True),
        halo(3, "wall", w, walls, own_one, one_after, False),
    ]
    for copy, sends, _ in halos:
        pl.when(sends)(copy.start)

    samples = dest_ref.shape[1]
    dest = dest_ref[...]
    across = jnp.broadcast_to(dest, (samples, samples))
    down = jnp.transpose(across)
    earlier = lax.broadcasted_iota(jnp.int32, (samples, samples), 0) < lax.broadcasted_iota(jnp.int32, (samples, samples), 1)
    slot = jnp.sum(jnp.where(jnp.logical_and(across == down, earlier), 1.0, 0.0), axis=0, keepdims=True)
    position = dest * CAP + slot.astype(jnp.int32)
    places = spans * CAP
    chosen = jnp.where(
        lax.broadcasted_iota(jnp.int32, (places, samples), 0) == position, 1.0, 0.0
    ).astype(jnp.bfloat16)
    wanted = jnp.dot(chosen, targets_ref[...], preferred_element_type=jnp.float32)
    flags = jnp.dot(chosen, jnp.ones((samples, samples), jnp.bfloat16), preferred_element_type=jnp.float32)
    marks_send[:, 0:CAP] = wanted.astype(jnp.bfloat16).reshape(spans, CAP, -1)
    marks_send[:, CAP : 2 * CAP] = flags.astype(jnp.bfloat16).reshape(spans, CAP, -1)

    def dispatch(send, held, send_sems, recv_sems):
        copies = []
        for d in range(1, spans):
            peer = lax.rem(i + d, spans)
            copies.append(
                pltpu.make_async_remote_copy(
                    src_ref=send.at[peer],
                    dst_ref=held.at[w, i],
                    send_sem=send_sems.at[d],
                    recv_sem=recv_sems.at[d],
                    device_id={"span": peer},
                    device_id_type=MESH,
                )
            )
        for copy in copies:
            copy.start()
        held[w, i] = send[i]
        return copies

    def arrive(held, copies, recv_sems, send_sems):
        for d in range(1, spans):
            source = lax.rem(i + spans - d, spans)
            pltpu.make_async_remote_copy(
                src_ref=held.at[w, source],
                dst_ref=held.at[w, source],
                send_sem=send_sems.at[d],
                recv_sem=recv_sems.at[d],
                device_id={"span": source},
                device_id_type=MESH,
            ).wait_recv()

    def gather(held, send_sems, recv_sems):
        copies = []
        for d in range(1, walls):
            copies.append(
                pltpu.make_async_remote_copy(
                    src_ref=held.at[w],
                    dst_ref=held.at[w],
                    send_sem=send_sems.at[d],
                    recv_sem=recv_sems.at[d],
                    device_id={"wall": lax.rem(w + d, walls)},
                    device_id_type=MESH,
                )
            )
        for copy in copies:
            copy.start()
        return copies

    def gathered(held, copies, send_sems, recv_sems):
        for d in range(1, walls):
            source = lax.rem(w + walls - d, walls)
            pltpu.make_async_remote_copy(
                src_ref=held.at[source],
                dst_ref=held.at[source],
                send_sem=send_sems.at[d],
                recv_sem=recv_sems.at[d],
                device_id={"wall": source},
                device_id_type=MESH,
            ).wait_recv()
        for copy in copies:
            copy.wait_send()

    marks_a = dispatch(marks_send, marks_all, marks_a_send, marks_a_recv)

    cells = cells_ref[...]
    picks = []
    for b in range(2):
        here = jnp.where(
            lax.broadcasted_iota(jnp.int32, (samples, samples), 0) + b * samples == cells, 1.0, 0.0
        ).astype(jnp.bfloat16)
        pick = lax.dot_general(
            chosen, here, (((1,), (1,)), ((), ())), preferred_element_type=jnp.float32
        )
        picks.append(pick.astype(jnp.bfloat16))

    loads[3].wait()
    means = [0.0, 0.0, 0.0]
    for m0 in RANGE:
        q = [field[m0, :, m] for m in RANGE]
        a = [velocity[2, m0, :, m] for m in RANGE]
        means[2] = means[2] + jnp.sum(a[0] + a[1] + a[2] + a[3] + a[4], axis=0)
        q_left, a_left, q_right, a_right = (
            weighted(LEFT, q), weighted(LEFT, a), weighted(RIGHT, q), weighted(RIGHT, a)
        )
        left = upwind(shift(q_right, 1), shift(a_right, 1), q_left, a_left)
        right = upwind(q_right, a_right, shift(q_left, -1), shift(a_left, -1))
        f = [x * y for x, y in zip(q, a)]
        for k in RANGE:
            new_ref[m0, :, k] = q[k] - (
                weighted(INNER[k], f)
                + left * np.float32(EDGE_LEFT[k])
                + right * np.float32(EDGE_RIGHT[k])
            )
    for m0 in RANGE:
        a = [velocity[1, m0, m] for m in RANGE]
        means[1] = means[1] + jnp.sum(a[0] + a[1] + a[2] + a[3] + a[4], axis=0)
        f = [field[m0, m] * a[m] for m in RANGE]
        for k in RANGE:
            new_ref[m0, k] = new_ref[m0, k] - weighted(INNER[k], f)
    for j in RANGE:
        a = [velocity[0, m, j] for m in RANGE]
        means[0] = means[0] + jnp.sum(a[0] + a[1] + a[2] + a[3] + a[4], axis=0)
        f = [field[m, j] * a[m] for m in RANGE]
        for k in RANGE:
            new_ref[k, j] = new_ref[k, j] - weighted(INNER[k], f)
    points = P_SIZE**3
    for d in range(3):
        flat[2 * (points + d) : 2 * (points + d) + 2] = means[d] * np.float32(1.0 / points)

    arrive(marks_all, marks_a, marks_a_recv, marks_a_send)
    marks_b = gather(marks_all, marks_b_send, marks_b_recv)

    for copy, _, gets in halos[:2]:
        pl.when(gets)(copy.wait_recv)
    for j in RANGE:
        left = upwind(zero_before[0, j], zero_before[1, j], own_zero[0, j], own_zero[1, j])
        right = upwind(own_zero[2, j], own_zero[3, j], zero_after[0, j], zero_after[1, j])
        for k in RANGE:
            new_ref[k, j] = new_ref[k, j] - (
                left * np.float32(EDGE_LEFT[k]) + right * np.float32(EDGE_RIGHT[k])
            )
    for copy, _, gets in halos[2:]:
        pl.when(gets)(copy.wait_recv)
    second = lax.broadcasted_iota(jnp.int32, (P_SIZE, 2, field.shape[-1]), 1) == 1
    for m0 in RANGE:
        before = [swap(jnp.where(second, one_before[n, m0], own_one[2 + n, m0])) for n in range(2)]
        after = [swap(jnp.where(second, own_one[n, m0], one_after[n, m0])) for n in range(2)]
        left = upwind(before[0], before[1], own_one[0, m0], own_one[1, m0])
        right = upwind(own_one[2, m0], own_one[3, m0], after[0], after[1])
        for k in RANGE:
            value = new_ref[m0, k] - (
                left * np.float32(EDGE_LEFT[k]) + right * np.float32(EDGE_RIGHT[k])
            )
            new_ref[m0, k] = value
            for n in RANGE:
                point = (m0 * P_SIZE + k) * P_SIZE + n
                flat[2 * point : 2 * point + 2] = value[n]

    total = None
    for b in range(2):
        values = flat[pl.ds(b, points + 3, stride=2)].astype(jnp.bfloat16)
        part = lax.dot_general(
            picks[b], values, (((1,), (1,)), ((), ())), preferred_element_type=jnp.float32
        )
        total = part if total is None else total + part
    rows_send[...] = total.astype(jnp.bfloat16).reshape(rows_send.shape)
    rows_a = dispatch(rows_send, rows_all, rows_a_send, rows_a_recv)
    arrive(rows_all, rows_a, rows_a_recv, rows_a_send)
    rows_b = gather(rows_all, rows_b_send, rows_b_recv)
    for copy, sends, _ in halos:
        pl.when(sends)(copy.wait_send)
    for copy in marks_a + rows_a:
        copy.wait_send()
    gathered(marks_all, marks_b, marks_b_send, marks_b_recv)
    gathered(rows_all, rows_b, rows_b_send, rows_b_recv)


def train_kernel(
    per_chunk,
    new_ref, rows_all, marks_all, one, two, three, four, five,
    new_out, grad_one, grad_two, grad_three, grad_four, grad_five,
    copy_sem,
):
    copy = pltpu.make_async_copy(new_ref, new_out, copy_sem)
    copy.start()
    walls, spans = rows_all.shape[:2]
    weights = (one, two, three, four, five)
    grads = (grad_one, grad_two, grad_three, grad_four, grad_five)
    chunks = walls // per_chunk
    count = per_chunk * spans * CAP

    def chunk(number):
        picked = pl.ds(number * per_chunk, per_chunk)
        act = rows_all[picked].reshape(count, -1)
        wanted = marks_all[picked, :, 0:CAP].reshape(per_chunk, spans * CAP, -1).astype(jnp.float32)
        flags = marks_all[picked, :, CAP : 2 * CAP].reshape(per_chunk, spans * CAP, -1).astype(jnp.float32)
        scale = flags / jnp.maximum(jnp.sum(flags, axis=1, keepdims=True), 1.0)
        acts = [act]
        slopes = []
        for layer in weights[:-1]:
            pre = jnp.dot(act, layer[0], preferred_element_type=jnp.float32)
            sigma = 0.5 + 0.5 * jnp.tanh(0.5 * pre)
            hidden = pre * sigma
            slopes.append(sigma + hidden * (1.0 - sigma))
            act = hidden.astype(jnp.bfloat16)
            acts.append(act)
        output = jnp.dot(act, weights[-1][0], preferred_element_type=jnp.float32)
        error = scale * (output.reshape(wanted.shape) - wanted)
        error = error.reshape(count, -1).astype(jnp.bfloat16)
        for layer in range(4, -1, -1):
            grad = lax.dot_general(
                acts[layer], error, (((0,), (0,)), ((), ())), preferred_element_type=jnp.float32
            )
            if chunks == 1:
                grads[layer][0] = grad
            else:
                grads[layer][0] += grad
            if layer:
                back = lax.dot_general(
                    error, weights[layer][0], (((1,), (1,)), ((), ())), preferred_element_type=jnp.float32
                )
                error = (back * slopes[layer - 1]).astype(jnp.bfloat16)

    if chunks == 1:
        chunk(0)
    else:
        for grad in grads:
            grad[...] = jnp.zeros_like(grad)
        pl.loop(0, chunks)(chunk)
    copy.wait()


def local(spans, walls, field, velocity, cells, destination, targets, *weights):
    shape = field.shape
    samples = cells.shape[0]
    inside = (P_SIZE, P_SIZE, P_SIZE, shape[3] * shape[4], shape[5])
    faces = (P_SIZE, P_SIZE) + inside[3:]
    vmem = pl.BlockSpec(memory_space=pltpu.VMEM)
    anywhere = pl.BlockSpec(memory_space=pl.ANY)
    features = P_SIZE**3 + 3
    wide = targets.shape[1]
    dma = pltpu.SemaphoreType.DMA
    new_field, rows_all, marks_all = pl.pallas_call(
        functools.partial(section_kernel, spans, walls),
        out_shape=(
            jax.ShapeDtypeStruct(inside, jnp.float32),
            jax.ShapeDtypeStruct((walls, spans, CAP, features), jnp.bfloat16),
            jax.ShapeDtypeStruct((walls, spans, 2 * CAP, wide), jnp.bfloat16),
        ),
        in_specs=[anywhere, anywhere, vmem, vmem, vmem],
        out_specs=(vmem, vmem, vmem),
        scratch_shapes=[
            pltpu.VMEM(inside, jnp.float32),
            pltpu.VMEM((3,) + inside, jnp.float32),
            pltpu.VMEM((4,) + faces, jnp.float32),
            pltpu.VMEM((4,) + faces, jnp.float32),
            pltpu.VMEM((2,) + faces, jnp.float32),
            pltpu.VMEM((2,) + faces, jnp.float32),
            pltpu.VMEM((2,) + faces, jnp.float32),
            pltpu.VMEM((2,) + faces, jnp.float32),
            pltpu.VMEM((2 * features, shape[5]), jnp.float32),
            pltpu.VMEM((spans, CAP, features), jnp.bfloat16),
            pltpu.VMEM((spans, 2 * CAP, wide), jnp.bfloat16),
            dma((4,)), dma((4,)), dma((4,)),
            dma((spans,)), dma((spans,)), dma((walls,)), dma((walls,)),
            dma((spans,)), dma((spans,)), dma((walls,)), dma((walls,)),
        ],
        compiler_params=pltpu.CompilerParams(
            collective_id=0, has_side_effects=True, vmem_limit_bytes=48 * 1024 * 1024
        ),
        name="section",
    )(
        field.reshape(inside),
        velocity.reshape((3,) + inside),
        cells.reshape(1, samples),
        destination.reshape(1, samples),
        targets,
    )
    per_chunk = max(1, min(walls, 512 // (spans * CAP)))
    while walls % per_chunk:
        per_chunk -= 1
    outs = pl.pallas_call(
        functools.partial(train_kernel, per_chunk),
        out_shape=(jax.ShapeDtypeStruct(inside, jnp.float32),)
        + tuple(jax.ShapeDtypeStruct(x.shape, jnp.float32) for x in weights),
        in_specs=[anywhere] + [vmem] * 7,
        out_specs=(anywhere,) + (vmem,) * 5,
        scratch_shapes=[dma(())],
        compiler_params=pltpu.CompilerParams(vmem_limit_bytes=48 * 1024 * 1024),
        name="train",
    )(new_field, rows_all, marks_all, *weights)
    return (outs[0].reshape(shape),) + tuple(outs[1:])


def solution(mesh):
    in_specs = (
        P(None, None, None, "span", "wall", None),
        P(None, None, None, None, "span", "wall", None),
        P(("span", "wall")),
        P(("span", "wall"), None),
        P(("span", "wall"), None),
        P("span", None, None),
        P("span", None, None),
        P("span", None, None),
        P("span", None, None),
        P("span", None, None),
    )
    out_specs = (
        P(None, None, None, "span", "wall", None),
        P("span", None, None),
        P("span", None, None),
        P("span", None, None),
        P("span", None, None),
        P("span", None, None),
    )
    body = functools.partial(local, mesh.shape["span"], mesh.shape["wall"])
    return jax.shard_map(body, mesh=mesh, in_specs=in_specs, out_specs=out_specs, check_vma=False)
```

time: 136 us -> 26 us (0.19)
  waiting for transfers between devices: 61.8 us -> 0 us
  starting transfers between devices: 24.1 us -> 0 us
  Pallas kernels: 0 us -> 21.7 us
  between operations: 15.4 us -> 0.72 us
  matrix products: 13.6 us -> 0 us
  local copies, waits for them, and re-layouts: 16 us -> 3.33 us
  other arithmetic: 4.08 us -> 0 us
    psum x1 -> x0, waiting for transfers between devices: 52.7 us -> none  [local(): lax.psum((grad_first, grad_second, grad_third, grad_fourth, grad_last), '...]
    pallas_call x0 -> x2, Pallas kernels: none -> 21.7 us  [the longest x1 19.2 us: local(): pl.pallas_call(functools.partial(section_kernel, spans, walls), out_shape...]
    all_to_all x3 -> x0, starting transfers between devices: 14.9 us -> none  [the longest x1 6.31 us: local(): lax.all_to_all(flag_buffer.reshape(span_count, slot_count), 'span', split...]
    dot_general x34 -> x0, matrix products: 13.6 us -> none  [the longest x18 6.38 us: at_face(): jnp.tensordot(vector, field, axes=([0], [axis]), precision=lax.Precision....]
    ppermute x4 -> x0, starting transfers between devices: 9.18 us -> none  [the longest x2 6.6 us: extended(): before = lax.ppermute(last, axis, up)]
    all_to_all x3 -> x0, waiting for transfers between devices: 9.14 us -> none  [the longest x1 5.64 us: local(): lax.all_to_all(row_buffer.reshape(span_count, slot_count, FEAT), 'span',...]
    unnamed x44 -> x20, local copies, waits for them, and re-layouts: 9.25 us -> 3.33 us
    scatter x2 -> x0, local copies, waits for them, and re-layouts: 3.02 us -> none  [the longest x1 1.68 us: local(): target_buffer = jnp.zeros((span_count * slot_count, targets.shape[1]), jn...]
  transfers between devices with their start and end apart: 8 -> 0, of which waited for: 3 -> 0; matrix products, arithmetic and copies ran while one was open for 10% -> 0% of each run, Pallas kernels for 0% -> 0%
where the time goes in v1:
time: 26 us; the launch traced here: 25.7 us
  Pallas kernels  21.7 us (83%)
  local copies, waits for them, and re-layouts  3.33 us (13%)
  between operations  0.72 us (3%)
    pallas_call x1, Pallas kernels, local(): pl.pallas_call(functools.partial(section_kernel, spans, walls), out_shape...  19.2 us
    unnamed x20, local copies, waits for them, and re-layouts  3.33 us
    pallas_call x1, Pallas kernels, local(): pl.pallas_call(functools.partial(train_kernel, per_chunk), out_shape=(jax...  2.47 us

profile of v1, /device:TPU:0, one launch (start us, length us, event | category | flops | bytes accessed | tf_op | source)
XLA Modules:
  0.0 25.7 jit_solution(7076886554082776063)
XLA Ops:
  0.6 0.0 copy-start.8
  0.6 0.0 copy-start.9
  0.7 0.6 %copy-done.8 = s32[128]{0:T(128)S(1)} copy-done((s32[128]{0:T(128)S(1)}, s32[128]{0:T(128)}, u32[]{:S(2)}) %copy-start.8) | copy-done | bytes 536
  1.3 0.0 copy-done.9
  1.3 0.0 copy-start
  1.3 1.0 %copy-done = f32[3,5,5,5,1,2,128]{6,5,4,3,2,1,0:T(2,128)S(1)} copy-done((f32[3,5,5,5,1,2,128]{6,5,4,3,2,1,0:T(2,128)S(1)}, f32[3,5,5,5,1,2,128]{6,5,4,3,2,1,0:T(2,128)}, u32[]{:S(2)}) %copy-start) | copy-done | bytes 384024
  2.3 0.0 copy-start.4
  2.3 0.9 %copy-done.4 = f32[5,5,5,1,2,128]{5,4,3,2,1,0:T(2,128)S(1)} copy-done((f32[5,5,5,1,2,128]{5,4,3,2,1,0:T(2,128)S(1)}, f32[5,5,5,1,2,128]{5,4,3,2,1,0:T(2,128)}, u32[]{:S(2)}) %copy-start.4) | copy-done | bytes 128024
  3.2 0.0 copy-start.7
  3.2 0.8 %copy-done.7 = bf16[128,128]{1,0:T(8,128)(2,1)S(1)} copy-done((bf16[128,128]{1,0:T(8,128)(2,1)S(1)}, bf16[128,128]{1,0:T(8,128)(2,1)}, u32[]{:S(2)}) %copy-start.7) | copy-done | bytes 32792
  4.0 0.0 copy-start.1
  4.0 0.0 copy-start.2
  4.0 0.0 copy-start.3
  4.0 0.0 copy-start.5
  4.0 0.0 copy-start.6
  4.0 19.2 %section.1 = (f32[5,5,5,2,128]{4,3,2,1,0:T(2,128)S(1)}, bf16[4,8,16,128]{3,2,1,0:T(8,128)(2,1)S(1)}, bf16[4,8,32,128]{3,2,1,0:T(8,128)(2,1)S(1)}) custom-call(f32[5,5,5,2,128]{4,3,2,1,0:T(2,128)S(1)} %bitcast.8, f32[3,5,5,5,2,128]{5,4,3,2,1,0:T(2,128)S(1)} %bitcast.7, s32[1,128]{1,0:T(1,128)S(1)} %bitcast.9, s32[1,128]{1,0:T(1,128)S(1)} %bitcast.10, ...), custom_call_target="tpu_custom_call" | custom-call | tf_op jit(solution)/shard_map/section/pallas_call | solution.py:424
  23.2 0.0 copy-done.1
  23.2 0.0 copy-done.2
  23.2 0.0 copy-done.3
  23.2 0.0 copy-done.5
  23.2 0.0 copy-done.6
  23.3 2.5 %train.1 = (f32[5,5,5,2,128]{4,3,2,1,0:T(2,128)}, f32[1,128,256]{2,1,0:T(8,128)}, f32[1,256,256]{2,1,0:T(8,128)}, f32[1,256,256]{2,1,0:T(8,128)}, f32[1,256,256]{2,1,0:T(8,128)}, /*index=5*/f32[1,256,128]{2,1,0:T(8,128)}) custom-call(f32[5,5,5,2,128]{4,3,2,1,0:T(2,128)S(1)} %get-tuple-element.15.new_ref, ...), custom_call_target="tpu_custom_call" | custom-call | tf_op jit(solution)/shard_map/train/pallas_call | solution.py:463
Async XLA Ops:
  0.6 0.7 %copy-start.8 = (s32[128]{0:T(128)S(1)}, s32[128]{0:T(128)}, u32[]{:S(2)}) copy-start(s32[128]{0:T(128)} %param.12) | copy-start | bytes 1540
  0.6 0.7 %copy-start.9 = (s32[128,1]{0,1:T(1,128)S(1)}, s32[128,1]{0,1:T(1,128)}, u32[]{:S(2)}) copy-start(s32[128,1]{0,1:T(1,128)} %param.13) | copy-start | bytes 1540
  1.3 1.0 %copy-start = (f32[3,5,5,5,1,2,128]{6,5,4,3,2,1,0:T(2,128)S(1)}, f32[3,5,5,5,1,2,128]{6,5,4,3,2,1,0:T(2,128)}, u32[]{:S(2)}) copy-start(f32[3,5,5,5,1,2,128]{6,5,4,3,2,1,0:T(2,128)} %param.11) | copy-start | bytes 1152004
  2.3 0.9 %copy-start.4 = (f32[5,5,5,1,2,128]{5,4,3,2,1,0:T(2,128)S(1)}, f32[5,5,5,1,2,128]{5,4,3,2,1,0:T(2,128)}, u32[]{:S(2)}) copy-start(f32[5,5,5,1,2,128]{5,4,3,2,1,0:T(2,128)} %param.10) | copy-start | bytes 384004
  3.2 0.8 %copy-start.7 = (bf16[128,128]{1,0:T(8,128)(2,1)S(1)}, bf16[128,128]{1,0:T(8,128)(2,1)}, u32[]{:S(2)}) copy-start(bf16[128,128]{1,0:T(8,128)(2,1)} %targets_ref.1) | copy-start | bytes 98308
  4.0 19.2 %copy-start.1 = (bf16[1,256,256]{2,1,0:T(8,128)(2,1)S(1)}, bf16[1,256,256]{2,1,0:T(8,128)(2,1)}, u32[]{:S(2)}) copy-start(bf16[1,256,256]{2,1,0:T(8,128)(2,1)} %two.1) | copy-start | bytes 393220
  4.0 19.3 %copy-start.2 = (bf16[1,256,256]{2,1,0:T(8,128)(2,1)S(1)}, bf16[1,256,256]{2,1,0:T(8,128)(2,1)}, u32[]{:S(2)}) copy-start(bf16[1,256,256]{2,1,0:T(8,128)(2,1)} %three.1) | copy-start | bytes 393220
  4.0 19.3 %copy-start.3 = (bf16[1,256,256]{2,1,0:T(8,128)(2,1)S(1)}, bf16[1,256,256]{2,1,0:T(8,128)(2,1)}, u32[]{:S(2)}) copy-start(bf16[1,256,256]{2,1,0:T(8,128)(2,1)} %four.1) | copy-start | bytes 393220
  4.0 19.3 %copy-start.5 = (bf16[1,128,256]{2,1,0:T(8,128)(2,1)S(1)}, bf16[1,128,256]{2,1,0:T(8,128)(2,1)}, u32[]{:S(2)}) copy-start(bf16[1,128,256]{2,1,0:T(8,128)(2,1)} %one.1) | copy-start | bytes 196612
  4.0 19.3 %copy-start.6 = (bf16[1,256,128]{2,1,0:T(8,128)(2,1)S(1)}, bf16[1,256,128]{2,1,0:T(8,128)(2,1)}, u32[]{:S(2)}) copy-start(bf16[1,256,128]{2,1,0:T(8,128)(2,1)} %five.1) | copy-start | bytes 196612

commit v2 on v1

--- a/solution.py
+++ b/solution.py
@@ -103,8 +103,9 @@
     return speed * (state_before + state_after) - jnp.abs(speed) * (state_after - state_before)
 
 
-def swap(x):
-    return jnp.concatenate([x[..., 1:2, :], x[..., 0:1, :]], axis=-2)
+def beside(x, y, row, other=None):
+    other = row if other is None else other
+    return jnp.concatenate([x[..., row : row + 1, :], y[..., other : other + 1, :]], axis=-2)
 
 
 def shift(x, step):
@@ -113,27 +114,30 @@
 
 def section_kernel(
     spans, walls,
-    field_hbm, velocity_hbm, cells_ref, dest_ref, targets_ref,
-    new_ref, rows_all, marks_all,
-    field, velocity, own_zero, own_one, zero_before, zero_after, one_before, one_after,
-    flat, rows_send, marks_send,
+    field_hbm, velocity_hbm, cells_hbm, dest_hbm, targets_hbm,
+    new_ref, rows_all, wanted_all, flags_all,
+    field, velocity, cells_ref, dest_ref, targets_ref,
+    own_zero, own_one, one_send, zero_before, zero_after, one_before, one_after,
+    flat, rows_send, marks_send, marks_held,
     in_sems, halo_send, halo_recv,
-    marks_a_send, marks_a_recv, marks_b_send, marks_b_recv,
+    marks_a_send, marks_a_recv, wanted_b_send, wanted_b_recv, flags_b_send, flags_b_recv,
     rows_a_send, rows_a_recv, rows_b_send, rows_b_recv,
 ):
     i = lax.axis_index("span")
     w = lax.axis_index("wall")
-    loads = [pltpu.make_async_copy(field_hbm, field, in_sems.at[0])]
-    for d in range(3):
-        loads.append(pltpu.make_async_copy(velocity_hbm.at[d], velocity.at[d], in_sems.at[1 + d]))
-    for load in loads:
-        load.start()
-
     barrier = pltpu.get_barrier_semaphore()
     for d in range(1, spans):
         pl.semaphore_signal(barrier, inc=1, device_id={"span": lax.rem(i + d, spans)}, device_id_type=MESH)
     for d in range(1, walls):
         pl.semaphore_signal(barrier, inc=1, device_id={"wall": lax.rem(w + d, walls)}, device_id_type=MESH)
+
+    loads = [pltpu.make_async_copy(field_hbm, field, in_sems.at[0])]
+    for d in range(3):
+        loads.append(pltpu.make_async_copy(velocity_hbm.at[d], velocity.at[d], in_sems.at[1 + d]))
+    for number, (whole, ref) in enumerate(((dest_hbm, dest_ref), (targets_hbm, targets_ref), (cells_hbm, cells_ref))):
+        loads.append(pltpu.make_async_copy(whole, ref, in_sems.at[4 + number]))
+    for load in loads:
+        load.start()
 
     for at_end, ref in ((i == 0, zero_before), (i == spans - 1, zero_after), (w == 0, one_before), (w == walls - 1, one_after)):
         @pl.when(at_end)
@@ -157,13 +161,15 @@
         own_one[1, m0] = weighted(LEFT, a)
         own_one[2, m0] = weighted(RIGHT, q)
         own_one[3, m0] = weighted(RIGHT, a)
+        one_send[0, m0] = beside(own_one[0, m0], own_one[1, m0], 0)
+        one_send[1, m0] = beside(own_one[2, m0], own_one[3, m0], 1)
 
     pl.semaphore_wait(barrier, spans + walls - 2)
 
-    def halo(number, axis, place, count, own, into, right):
+    def halo(number, axis, place, count, source, into, right):
         peer = jnp.minimum(place + 1, count - 1) if right else jnp.maximum(place - 1, 0)
         copy = pltpu.make_async_remote_copy(
-            src_ref=own.at[pl.ds(2 if right else 0, 2)],
+            src_ref=source,
             dst_ref=into,
             send_sem=halo_send.at[number],
             recv_sem=halo_recv.at[number],
@@ -175,15 +181,17 @@
         return copy, sends, gets
 
     halos = [
-        halo(0, "span", i, spans, own_zero, zero_before, True),
-        halo(1, "span", i, spans, own_zero, zero_after, False),
-        halo(2, "wall", w, walls, own_one, one_before, True),
-        halo(3, "wall", w, walls, own_one, one_after, False),
+        halo(0, "span", i, spans, own_zero.at[2:4], zero_before, True),
+        halo(1, "span", i, spans, own_zero.at[0:2], zero_after, False),
+        halo(2, "wall", w, walls, one_send.at[1], one_before, True),
+        halo(3, "wall", w, walls, one_send.at[0], one_after, False),
     ]
     for copy, sends, _ in halos:
         pl.when(sends)(copy.start)
 
     samples = dest_ref.shape[1]
+    for load in loads[4:]:
+        load.wait()
     dest = dest_ref[...]
     across = jnp.broadcast_to(dest, (samples, samples))
     down = jnp.transpose(across)
@@ -206,7 +214,7 @@
             copies.append(
                 pltpu.make_async_remote_copy(
                     src_ref=send.at[peer],
-                    dst_ref=held.at[w, i],
+                    dst_ref=held.at[i],
                     send_sem=send_sems.at[d],
                     recv_sem=recv_sems.at[d],
                     device_id={"span": peer},
@@ -215,15 +223,15 @@
             )
         for copy in copies:
             copy.start()
-        held[w, i] = send[i]
+        held[i] = send[i]
         return copies
 
-    def arrive(held, copies, recv_sems, send_sems):
+    def arrive(held, send_sems, recv_sems):
         for d in range(1, spans):
             source = lax.rem(i + spans - d, spans)
             pltpu.make_async_remote_copy(
-                src_ref=held.at[w, source],
-                dst_ref=held.at[w, source],
+                src_ref=held.at[source],
+                dst_ref=held.at[source],
                 send_sem=send_sems.at[d],
                 recv_sem=recv_sems.at[d],
                 device_id={"span": source},
@@ -261,7 +269,7 @@
         for copy in copies:
             copy.wait_send()
 
-    marks_a = dispatch(marks_send, marks_all, marks_a_send, marks_a_recv)
+    marks_a = dispatch(marks_send, marks_held, marks_a_send, marks_a_recv)
 
     cells = cells_ref[...]
     picks = []
@@ -308,8 +316,12 @@
     for d in range(3):
         flat[2 * (points + d) : 2 * (points + d) + 2] = means[d] * np.float32(1.0 / points)
 
-    arrive(marks_all, marks_a, marks_a_recv, marks_a_send)
-    marks_b = gather(marks_all, marks_b_send, marks_b_recv)
+    arrive(marks_held, marks_a_send, marks_a_recv)
+    wanted_all[w] = marks_held[:, 0:CAP].reshape(places, -1)
+    flags_here = marks_held[:, CAP : 2 * CAP].reshape(places, -1).astype(jnp.float32)
+    flags_all[w] = jnp.transpose(flags_here)[0:CAP].astype(jnp.bfloat16)
+    wanted_b = gather(wanted_all, wanted_b_send, wanted_b_recv)
+    flags_b = gather(flags_all, flags_b_send, flags_b_recv)
 
     for copy, _, gets in halos[:2]:
         pl.when(gets)(copy.wait_recv)
@@ -322,10 +334,9 @@
             )
     for copy, _, gets in halos[2:]:
         pl.when(gets)(copy.wait_recv)
-    second = lax.broadcasted_iota(jnp.int32, (P_SIZE, 2, field.shape[-1]), 1) == 1
     for m0 in RANGE:
-        before = [swap(jnp.where(second, one_before[n, m0], own_one[2 + n, m0])) for n in range(2)]
-        after = [swap(jnp.where(second, own_one[n, m0], one_after[n, m0])) for n in range(2)]
+        before = [beside(one_before[m0], own_one[2 + n, m0], n, 0) for n in range(2)]
+        after = [beside(own_one[n, m0], one_after[m0], 1, n) for n in range(2)]
         left = upwind(before[0], before[1], own_one[0, m0], own_one[1, m0])
         right = upwind(own_one[2, m0], own_one[3, m0], after[0], after[1])
         for k in RANGE:
@@ -345,37 +356,50 @@
         )
         total = part if total is None else total + part
     rows_send[...] = total.astype(jnp.bfloat16).reshape(rows_send.shape)
-    rows_a = dispatch(rows_send, rows_all, rows_a_send, rows_a_recv)
-    arrive(rows_all, rows_a, rows_a_recv, rows_a_send)
+    rows_a = dispatch(rows_send, rows_all.at[w], rows_a_send, rows_a_recv)
+    arrive(rows_all.at[w], rows_a_send, rows_a_recv)
     rows_b = gather(rows_all, rows_b_send, rows_b_recv)
     for copy, sends, _ in halos:
         pl.when(sends)(copy.wait_send)
     for copy in marks_a + rows_a:
         copy.wait_send()
-    gathered(marks_all, marks_b, marks_b_send, marks_b_recv)
+    gathered(wanted_all, wanted_b, wanted_b_send, wanted_b_recv)
+    gathered(flags_all, flags_b, flags_b_send, flags_b_recv)
     gathered(rows_all, rows_b, rows_b_send, rows_b_recv)
 
 
 def train_kernel(
     per_chunk,
-    new_ref, rows_all, marks_all, one, two, three, four, five,
-    new_out, grad_one, grad_two, grad_three, grad_four, grad_five,
-    copy_sem,
+    new_ref, rows_all, wanted_all, flags_all, one, two, three, four, five,
+    new_out, out_one, out_two, out_three, out_four, out_five,
+    grad_one, grad_two, grad_three, grad_four, grad_five, sems,
 ):
-    copy = pltpu.make_async_copy(new_ref, new_out, copy_sem)
-    copy.start()
+    copies = [pltpu.make_async_copy(new_ref, new_out, sems.at[5])]
+    copies[0].start()
     walls, spans = rows_all.shape[:2]
     weights = (one, two, three, four, five)
     grads = (grad_one, grad_two, grad_three, grad_four, grad_five)
+    outs = (out_one, out_two, out_three, out_four, out_five)
     chunks = walls // per_chunk
-    count = per_chunk * spans * CAP
+    places = spans * CAP
+    count = per_chunk * places
+
+    def leave(layer):
+        copy = pltpu.make_async_copy(grads[layer], outs[layer], sems.at[layer])
+        copy.start()
+        copies.append(copy)
 
     def chunk(number):
-        picked = pl.ds(number * per_chunk, per_chunk)
-        act = rows_all[picked].reshape(count, -1)
-        wanted = marks_all[picked, :, 0:CAP].reshape(per_chunk, spans * CAP, -1).astype(jnp.float32)
-        flags = marks_all[picked, :, CAP : 2 * CAP].reshape(per_chunk, spans * CAP, -1).astype(jnp.float32)
-        scale = flags / jnp.maximum(jnp.sum(flags, axis=1, keepdims=True), 1.0)
+        first = number * per_chunk
+        act = rows_all[pl.ds(first, per_chunk)].reshape(count, -1)
+        wanted = wanted_all[pl.ds(first, per_chunk)].reshape(count, -1).astype(jnp.float32)
+        wide = wanted.shape[1]
+        scales = []
+        for n in range(per_chunk):
+            flags = flags_all[first + n].astype(jnp.float32)[0:1]
+            scale = flags / jnp.maximum(jnp.sum(flags, axis=1, keepdims=True), 1.0)
+            scales.append(jnp.transpose(jnp.broadcast_to(scale, (wide, places))))
+        scale = scales[0] if per_chunk == 1 else jnp.concatenate(scales, axis=0)
         acts = [act]
         slopes = []
         for layer in weights[:-1]:
@@ -386,14 +410,14 @@
             act = hidden.astype(jnp.bfloat16)
             acts.append(act)
         output = jnp.dot(act, weights[-1][0], preferred_element_type=jnp.float32)
-        error = scale * (output.reshape(wanted.shape) - wanted)
-        error = error.reshape(count, -1).astype(jnp.bfloat16)
+        error = (scale * (output - wanted)).astype(jnp.bfloat16)
         for layer in range(4, -1, -1):
             grad = lax.dot_general(
                 acts[layer], error, (((0,), (0,)), ((), ())), preferred_element_type=jnp.float32
             )
             if chunks == 1:
                 grads[layer][0] = grad
+                leave(layer)
             else:
                 grads[layer][0] += grad
             if layer:
@@ -408,7 +432,10 @@
         for grad in grads:
             grad[...] = jnp.zeros_like(grad)
         pl.loop(0, chunks)(chunk)
-    copy.wait()
+        for layer in range(5):
+            leave(layer)
+    for copy in copies:
+        copy.wait()
 
 
 def local(spans, walls, field, velocity, cells, destination, targets, *weights):
@@ -418,32 +445,39 @@
     faces = (P_SIZE, P_SIZE) + inside[3:]
     vmem = pl.BlockSpec(memory_space=pltpu.VMEM)
     anywhere = pl.BlockSpec(memory_space=pl.ANY)
+    hbm = pl.BlockSpec(memory_space=pltpu.HBM)
     features = P_SIZE**3 + 3
     wide = targets.shape[1]
     dma = pltpu.SemaphoreType.DMA
-    new_field, rows_all, marks_all = pl.pallas_call(
+    new_field, *received = pl.pallas_call(
         functools.partial(section_kernel, spans, walls),
         out_shape=(
             jax.ShapeDtypeStruct(inside, jnp.float32),
             jax.ShapeDtypeStruct((walls, spans, CAP, features), jnp.bfloat16),
-            jax.ShapeDtypeStruct((walls, spans, 2 * CAP, wide), jnp.bfloat16),
+            jax.ShapeDtypeStruct((walls, spans * CAP, wide), jnp.bfloat16),
+            jax.ShapeDtypeStruct((walls, CAP, spans * CAP), jnp.bfloat16),
         ),
-        in_specs=[anywhere, anywhere, vmem, vmem, vmem],
-        out_specs=(vmem, vmem, vmem),
+        in_specs=[hbm] * 5,
+        out_specs=(vmem,) * 4,
         scratch_shapes=[
             pltpu.VMEM(inside, jnp.float32),
             pltpu.VMEM((3,) + inside, jnp.float32),
+            pltpu.VMEM((1, samples), jnp.int32),
+            pltpu.VMEM((1, samples), jnp.int32),
+            pltpu.VMEM(targets.shape, jnp.bfloat16),
             pltpu.VMEM((4,) + faces, jnp.float32),
             pltpu.VMEM((4,) + faces, jnp.float32),
             pltpu.VMEM((2,) + faces, jnp.float32),
             pltpu.VMEM((2,) + faces, jnp.float32),
             pltpu.VMEM((2,) + faces, jnp.float32),
-            pltpu.VMEM((2,) + faces, jnp.float32),
+            pltpu.VMEM(faces, jnp.float32),
+            pltpu.VMEM(faces, jnp.float32),
             pltpu.VMEM((2 * features, shape[5]), jnp.float32),
             pltpu.VMEM((spans, CAP, features), jnp.bfloat16),
             pltpu.VMEM((spans, 2 * CAP, wide), jnp.bfloat16),
-            dma((4,)), dma((4,)), dma((4,)),
-            dma((spans,)), dma((spans,)), dma((walls,)), dma((walls,)),
+            pltpu.VMEM((spans, 2 * CAP, wide), jnp.bfloat16),
+            dma((7,)), dma((4,)), dma((4,)),
+            dma((spans,)), dma((spans,)), dma((walls,)), dma((walls,)), dma((walls,)), dma((walls,)),
             dma((spans,)), dma((spans,)), dma((walls,)), dma((walls,)),
         ],
         compiler_params=pltpu.CompilerParams(
@@ -451,11 +485,16 @@
         ),
         name="section",
     )(
-        field.reshape(inside),
-        velocity.reshape((3,) + inside),
-        cells.reshape(1, samples),
-        destination.reshape(1, samples),
-        targets,
+        *(
+            pltpu.with_memory_space_constraint(x, pltpu.HBM)
+            for x in (
+                field.reshape(inside),
+                velocity.reshape((3,) + inside),
+                cells.reshape(1, samples),
+                destination.reshape(1, samples),
+                targets,
+            )
+        )
     )
     per_chunk = max(1, min(walls, 512 // (spans * CAP)))
     while walls % per_chunk:
@@ -464,12 +503,12 @@
         functools.partial(train_kernel, per_chunk),
         out_shape=(jax.ShapeDtypeStruct(inside, jnp.float32),)
         + tuple(jax.ShapeDtypeStruct(x.shape, jnp.float32) for x in weights),
-        in_specs=[anywhere] + [vmem] * 7,
-        out_specs=(anywhere,) + (vmem,) * 5,
-        scratch_shapes=[dma(())],
+        in_specs=[anywhere] + [vmem] * 8,
+        out_specs=(anywhere,) * 6,
+        scratch_shapes=[pltpu.VMEM(x.shape, jnp.float32) for x in weights] + [dma((6,))],
         compiler_params=pltpu.CompilerParams(vmem_limit_bytes=48 * 1024 * 1024),
         name="train",
-    )(new_field, rows_all, marks_all, *weights)
+    )(new_field, *received, *weights)
     return (outs[0].reshape(shape),) + tuple(outs[1:])
 
 

time: 26 us -> 21.8 us (0.84)
  local copies, waits for them, and re-layouts: 3.33 us -> 0.02 us
  Pallas kernels: 21.7 us -> 20.9 us
    unnamed x20 -> x10, local copies, waits for them, and re-layouts: 3.33 us -> 0.02 us
    pallas_call x1, Pallas kernels: 19.2 us -> 18.7 us  [local(): pl.pallas_call(functools.partial(section_kernel, spans, walls), out_shape...]
where the time goes in v2:
time: 21.8 us; the launch traced here: 21.7 us
  Pallas kernels  20.9 us (96%)
  between operations  0.72 us (3%)
    pallas_call x1, Pallas kernels, local(): pl.pallas_call(functools.partial(section_kernel, spans, walls), out_shape...  18.7 us
    pallas_call x1, Pallas kernels, local(): pl.pallas_call(functools.partial(train_kernel, per_chunk), out_shape=(jax...  2.21 us

profile of v2, /device:TPU:0, one launch (start us, length us, event | category | flops | bytes accessed | tf_op | source)
XLA Modules:
  0.0 21.7 jit_solution(17562202268472850259)
XLA Ops:
  0.6 0.0 copy-start
  0.6 0.0 copy-start.1
  0.7 0.0 copy-start.2
  0.7 0.0 copy-start.3
  0.7 0.0 copy-start.4
  0.7 18.7 %section.1 = (f32[5,5,5,2,128]{4,3,2,1,0:T(2,128)S(1)}, bf16[4,8,16,128]{3,2,1,0:T(8,128)(2,1)S(1)}, bf16[4,128,128]{2,1,0:T(8,128)(2,1)S(1)}, bf16[4,16,128]{2,1,0:T(8,128)(2,1)S(1)}) custom-call(f32[5,5,5,2,128]{4,3,2,1,0:T(2,128)} %bitcast.8, f32[3,5,5,5,2,128]{5,4,3,2,1,0:T(2,128)} %bitcast.7, s32[1,128]{1,0:T(1,128)} %bitcast.9, s32[1,128]{1,0:T(1,128)} %bitcast.10, ...), custom_call_target="tpu_custom_call" | custom-call | tf_op jit(solution)/shard_map/section/pallas_call | solution.py:452
  19.4 0.0 copy-done
  19.4 0.0 copy-done.1
  19.4 0.0 copy-done.2
  19.4 0.0 copy-done.3
  19.5 0.0 copy-done.4
  19.5 2.2 %train.1 = (f32[5,5,5,2,128]{4,3,2,1,0:T(2,128)}, f32[1,128,256]{2,1,0:T(8,128)}, f32[1,256,256]{2,1,0:T(8,128)}, f32[1,256,256]{2,1,0:T(8,128)}, f32[1,256,256]{2,1,0:T(8,128)}, /*index=5*/f32[1,256,128]{2,1,0:T(8,128)}) custom-call(f32[5,5,5,2,128]{4,3,2,1,0:T(2,128)S(1)} %get-tuple-element.16.new_ref, ...), custom_call_target="tpu_custom_call" | custom-call | tf_op jit(solution)/shard_map/train/pallas_call | solution.py:502
Async XLA Ops:
  0.6 18.8 %copy-start = (bf16[1,256,256]{2,1,0:T(8,128)(2,1)S(1)}, bf16[1,256,256]{2,1,0:T(8,128)(2,1)}, u32[]{:S(2)}) copy-start(bf16[1,256,256]{2,1,0:T(8,128)(2,1)} %two.1) | copy-start | bytes 393220
  0.6 18.8 %copy-start.1 = (bf16[1,256,256]{2,1,0:T(8,128)(2,1)S(1)}, bf16[1,256,256]{2,1,0:T(8,128)(2,1)}, u32[]{:S(2)}) copy-start(bf16[1,256,256]{2,1,0:T(8,128)(2,1)} %three.1) | copy-start | bytes 393220
  0.7 18.8 %copy-start.2 = (bf16[1,256,256]{2,1,0:T(8,128)(2,1)S(1)}, bf16[1,256,256]{2,1,0:T(8,128)(2,1)}, u32[]{:S(2)}) copy-start(bf16[1,256,256]{2,1,0:T(8,128)(2,1)} %four.1) | copy-start | bytes 393220
  0.7 18.8 %copy-start.3 = (bf16[1,128,256]{2,1,0:T(8,128)(2,1)S(1)}, bf16[1,128,256]{2,1,0:T(8,128)(2,1)}, u32[]{:S(2)}) copy-start(bf16[1,128,256]{2,1,0:T(8,128)(2,1)} %one.1) | copy-start | bytes 196612
  0.7 18.8 %copy-start.4 = (bf16[1,256,128]{2,1,0:T(8,128)(2,1)S(1)}, bf16[1,256,128]{2,1,0:T(8,128)(2,1)}, u32[]{:S(2)}) copy-start(bf16[1,256,128]{2,1,0:T(8,128)(2,1)} %five.1) | copy-start | bytes 196612

commit v3 on v2

--- a/solution.py
+++ b/solution.py
@@ -108,6 +108,19 @@
     return jnp.concatenate([x[..., row : row + 1, :], y[..., other : other + 1, :]], axis=-2)
 
 
+def paired(place, d):
+    bit = 1
+    while bit <= d:
+        if d & bit:
+            place = place + bit * (1 - 2 * lax.rem(lax.div(place, bit), 2))
+        bit *= 2
+    return place
+
+
+def is_full(spans, samples):
+    return spans * CAP == samples
+
+
 def shift(x, step):
     return jnp.concatenate([x[..., -step:], x[..., :-step]], axis=-1)
 
@@ -115,13 +128,12 @@
 def section_kernel(
     spans, walls,
     field_hbm, velocity_hbm, cells_hbm, dest_hbm, targets_hbm,
-    new_ref, rows_all, wanted_all, flags_all,
+    new_ref, rows_all, marks_all,
     field, velocity, cells_ref, dest_ref, targets_ref,
     own_zero, own_one, one_send, zero_before, zero_after, one_before, one_after,
-    flat, rows_send, marks_send, marks_held,
+    flat, rows_send, marks_send,
     in_sems, halo_send, halo_recv,
-    marks_a_send, marks_a_recv, wanted_b_send, wanted_b_recv, flags_b_send, flags_b_recv,
-    rows_a_send, rows_a_recv, rows_b_send, rows_b_recv,
+    marks_sems, marks_wall_sems, rows_sems, rows_wall_sems,
 ):
     i = lax.axis_index("span")
     w = lax.axis_index("wall")
@@ -203,73 +215,83 @@
         lax.broadcasted_iota(jnp.int32, (places, samples), 0) == position, 1.0, 0.0
     ).astype(jnp.bfloat16)
     wanted = jnp.dot(chosen, targets_ref[...], preferred_element_type=jnp.float32)
-    flags = jnp.dot(chosen, jnp.ones((samples, samples), jnp.bfloat16), preferred_element_type=jnp.float32)
     marks_send[:, 0:CAP] = wanted.astype(jnp.bfloat16).reshape(spans, CAP, -1)
-    marks_send[:, CAP : 2 * CAP] = flags.astype(jnp.bfloat16).reshape(spans, CAP, -1)
-
-    def dispatch(send, held, send_sems, recv_sems):
+    if not is_full(spans, samples):
+        flags = jnp.dot(chosen, jnp.ones((samples, samples), jnp.bfloat16), preferred_element_type=jnp.float32)
+        marks_send[:, CAP : 2 * CAP] = flags.astype(jnp.bfloat16).reshape(spans, CAP, -1)
+
+    groups = min(spans, 8)
+    size = spans // groups
+
+    def group_of(held, wall, g):
+        return held.at[wall, pl.ds(paired(lax.div(i, size), g) * size, size)]
+
+    def dispatch(send, held, sems, wall_sems):
+        copies = [
+            pltpu.make_async_remote_copy(
+                src_ref=send.at[paired(i, d)],
+                dst_ref=held.at[w, i],
+                send_sem=sems.at[0, d],
+                recv_sem=sems.at[1, d],
+                device_id={"span": paired(i, d)},
+                device_id_type=MESH,
+            )
+            for d in range(1, spans)
+        ]
+        for copy in copies:
+            copy.start()
+        held[w, i] = send[i]
+        if size == 1:
+            copies = copies + forward(held, wall_sems, 0)
+        return copies
+
+    def forward(held, sems, g):
+        place = group_of(held, w, g)
+        copies = [
+            pltpu.make_async_remote_copy(
+                src_ref=place,
+                dst_ref=place,
+                send_sem=sems.at[0, n, g],
+                recv_sem=sems.at[1, n, g],
+                device_id={"wall": paired(w, n)},
+                device_id_type=MESH,
+            )
+            for n in range(1, walls)
+        ]
+        for copy in copies:
+            copy.start()
+        return copies
+
+    def pass_on(held, sems, wall_sems):
         copies = []
         for d in range(1, spans):
-            peer = lax.rem(i + d, spans)
-            copies.append(
-                pltpu.make_async_remote_copy(
-                    src_ref=send.at[peer],
-                    dst_ref=held.at[i],
-                    send_sem=send_sems.at[d],
-                    recv_sem=recv_sems.at[d],
-                    device_id={"span": peer},
-                    device_id_type=MESH,
-                )
-            )
-        for copy in copies:
-            copy.start()
-        held[i] = send[i]
-        return copies
-
-    def arrive(held, send_sems, recv_sems):
-        for d in range(1, spans):
-            source = lax.rem(i + spans - d, spans)
+            source = paired(i, d)
             pltpu.make_async_remote_copy(
-                src_ref=held.at[source],
-                dst_ref=held.at[source],
-                send_sem=send_sems.at[d],
-                recv_sem=recv_sems.at[d],
+                src_ref=held.at[w, source],
+                dst_ref=held.at[w, source],
+                send_sem=sems.at[0, d],
+                recv_sem=sems.at[1, d],
                 device_id={"span": source},
                 device_id_type=MESH,
             ).wait_recv()
-
-    def gather(held, send_sems, recv_sems):
-        copies = []
-        for d in range(1, walls):
-            copies.append(
+            if (d + 1) % size == 0:
+                copies += forward(held, wall_sems, d // size)
+        return copies
+
+    def finish(held, sems):
+        for g in range(groups):
+            for n in range(1, walls):
+                place = group_of(held, paired(w, n), g)
                 pltpu.make_async_remote_copy(
-                    src_ref=held.at[w],
-                    dst_ref=held.at[w],
-                    send_sem=send_sems.at[d],
-                    recv_sem=recv_sems.at[d],
-                    device_id={"wall": lax.rem(w + d, walls)},
+                    src_ref=place,
+                    dst_ref=place,
+                    send_sem=sems.at[0, n, g],
+                    recv_sem=sems.at[1, n, g],
+                    device_id={"wall": paired(w, n)},
                     device_id_type=MESH,
-                )
-            )
-        for copy in copies:
-            copy.start()
-        return copies
-
-    def gathered(held, copies, send_sems, recv_sems):
-        for d in range(1, walls):
-            source = lax.rem(w + walls - d, walls)
-            pltpu.make_async_remote_copy(
-                src_ref=held.at[source],
-                dst_ref=held.at[source],
-                send_sem=send_sems.at[d],
-                recv_sem=recv_sems.at[d],
-                device_id={"wall": source},
-                device_id_type=MESH,
-            ).wait_recv()
-        for copy in copies:
-            copy.wait_send()
-
-    marks_a = dispatch(marks_send, marks_held, marks_a_send, marks_a_recv)
+                ).wait_recv()
+
+    sent = dispatch(marks_send, marks_all, marks_sems, marks_wall_sems)
 
     cells = cells_ref[...]
     picks = []
@@ -316,12 +338,7 @@
     for d in range(3):
         flat[2 * (points + d) : 2 * (points + d) + 2] = means[d] * np.float32(1.0 / points)
 
-    arrive(marks_held, marks_a_send, marks_a_recv)
-    wanted_all[w] = marks_held[:, 0:CAP].reshape(places, -1)
-    flags_here = marks_held[:, CAP : 2 * CAP].reshape(places, -1).astype(jnp.float32)
-    flags_all[w] = jnp.transpose(flags_here)[0:CAP].astype(jnp.bfloat16)
-    wanted_b = gather(wanted_all, wanted_b_send, wanted_b_recv)
-    flags_b = gather(flags_all, flags_b_send, flags_b_recv)
+    sent += pass_on(marks_all, marks_sems, marks_wall_sems)
 
     for copy, _, gets in halos[:2]:
         pl.when(gets)(copy.wait_recv)
@@ -356,21 +373,19 @@
         )
         total = part if total is None else total + part
     rows_send[...] = total.astype(jnp.bfloat16).reshape(rows_send.shape)
-    rows_a = dispatch(rows_send, rows_all.at[w], rows_a_send, rows_a_recv)
-    arrive(rows_all.at[w], rows_a_send, rows_a_recv)
-    rows_b = gather(rows_all, rows_b_send, rows_b_recv)
+    sent += dispatch(rows_send, rows_all, rows_sems, rows_wall_sems)
+    sent += pass_on(rows_all, rows_sems, rows_wall_sems)
     for copy, sends, _ in halos:
         pl.when(sends)(copy.wait_send)
-    for copy in marks_a + rows_a:
+    for copy in sent:
         copy.wait_send()
-    gathered(wanted_all, wanted_b, wanted_b_send, wanted_b_recv)
-    gathered(flags_all, flags_b, flags_b_send, flags_b_recv)
-    gathered(rows_all, rows_b, rows_b_send, rows_b_recv)
+    finish(marks_all, marks_wall_sems)
+    finish(rows_all, rows_wall_sems)
 
 
 def train_kernel(
-    per_chunk,
-    new_ref, rows_all, wanted_all, flags_all, one, two, three, four, five,
+    per_chunk, full,
+    new_ref, rows_all, marks_all, one, two, three, four, five,
     new_out, out_one, out_two, out_three, out_four, out_five,
     grad_one, grad_two, grad_three, grad_four, grad_five, sems,
 ):
@@ -392,14 +407,14 @@
     def chunk(number):
         first = number * per_chunk
         act = rows_all[pl.ds(first, per_chunk)].reshape(count, -1)
-        wanted = wanted_all[pl.ds(first, per_chunk)].reshape(count, -1).astype(jnp.float32)
-        wide = wanted.shape[1]
-        scales = []
-        for n in range(per_chunk):
-            flags = flags_all[first + n].astype(jnp.float32)[0:1]
+        picked = marks_all.at[pl.ds(first, per_chunk)]
+        wanted = picked[:, :, 0:CAP].reshape(count, -1).astype(jnp.float32)
+        if full:
+            scale = np.float32(1.0 / places)
+        else:
+            flags = picked[:, :, CAP : 2 * CAP].reshape(per_chunk, places, -1).astype(jnp.float32)
             scale = flags / jnp.maximum(jnp.sum(flags, axis=1, keepdims=True), 1.0)
-            scales.append(jnp.transpose(jnp.broadcast_to(scale, (wide, places))))
-        scale = scales[0] if per_chunk == 1 else jnp.concatenate(scales, axis=0)
+            scale = scale.reshape(count, -1)
         acts = [act]
         slopes = []
         for layer in weights[:-1]:
@@ -448,17 +463,18 @@
     hbm = pl.BlockSpec(memory_space=pltpu.HBM)
     features = P_SIZE**3 + 3
     wide = targets.shape[1]
+    full = is_full(spans, samples)
+    marks = CAP if full else 2 * CAP
     dma = pltpu.SemaphoreType.DMA
     new_field, *received = pl.pallas_call(
         functools.partial(section_kernel, spans, walls),
         out_shape=(
             jax.ShapeDtypeStruct(inside, jnp.float32),
             jax.ShapeDtypeStruct((walls, spans, CAP, features), jnp.bfloat16),
-            jax.ShapeDtypeStruct((walls, spans * CAP, wide), jnp.bfloat16),
-            jax.ShapeDtypeStruct((walls, CAP, spans * CAP), jnp.bfloat16),
+            jax.ShapeDtypeStruct((walls, spans, marks, wide), jnp.bfloat16),
         ),
         in_specs=[hbm] * 5,
-        out_specs=(vmem,) * 4,
+        out_specs=(vmem,) * 3,
         scratch_shapes=[
             pltpu.VMEM(inside, jnp.float32),
             pltpu.VMEM((3,) + inside, jnp.float32),
@@ -474,11 +490,9 @@
             pltpu.VMEM(faces, jnp.float32),
             pltpu.VMEM((2 * features, shape[5]), jnp.float32),
             pltpu.VMEM((spans, CAP, features), jnp.bfloat16),
-            pltpu.VMEM((spans, 2 * CAP, wide), jnp.bfloat16),
-            pltpu.VMEM((spans, 2 * CAP, wide), jnp.bfloat16),
+            pltpu.VMEM((spans, marks, wide), jnp.bfloat16),
             dma((7,)), dma((4,)), dma((4,)),
-            dma((spans,)), dma((spans,)), dma((walls,)), dma((walls,)), dma((walls,)), dma((walls,)),
-            dma((spans,)), dma((spans,)), dma((walls,)), dma((walls,)),
+            dma((2, spans)), dma((2, walls, min(spans, 8))), dma((2, spans)), dma((2, walls, min(spans, 8))),
         ],
         compiler_params=pltpu.CompilerParams(
             collective_id=0, has_side_effects=True, vmem_limit_bytes=48 * 1024 * 1024
@@ -500,10 +514,10 @@
     while walls % per_chunk:
         per_chunk -= 1
     outs = pl.pallas_call(
-        functools.partial(train_kernel, per_chunk),
+        functools.partial(train_kernel, per_chunk, full),
         out_shape=(jax.ShapeDtypeStruct(inside, jnp.float32),)
         + tuple(jax.ShapeDtypeStruct(x.shape, jnp.float32) for x in weights),
-        in_specs=[anywhere] + [vmem] * 8,
+        in_specs=[anywhere] + [vmem] * 7,
         out_specs=(anywhere,) * 6,
         scratch_shapes=[pltpu.VMEM(x.shape, jnp.float32) for x in weights] + [dma((6,))],
         compiler_params=pltpu.CompilerParams(vmem_limit_bytes=48 * 1024 * 1024),

time: 21.8 us -> 22.1 us (1.014)
  Pallas kernels: 20.9 us -> 21.2 us
    pallas_call x1, Pallas kernels: 18.7 us -> 18.9 us  [local(): pl.pallas_call(functools.partial(section_kernel, spans, walls), out_shape...]
where the time goes in v3:
time: 22.1 us; the launch traced here: 21.9 us
  Pallas kernels  21.2 us (96%)
  between operations  0.72 us (3%)
    pallas_call x1, Pallas kernels, local(): pl.pallas_call(functools.partial(section_kernel, spans, walls), out_shape...  18.9 us
    pallas_call x1, Pallas kernels, local(): pl.pallas_call(functools.partial(train_kernel, per_chunk, full), out_shap...  2.21 us

profile of v3, /device:TPU:0, one launch (start us, length us, event | category | flops | bytes accessed | tf_op | source)
XLA Modules:
  0.0 21.9 jit_solution(14073947312232688236)
XLA Ops:
  0.6 0.0 copy-start
  0.6 0.0 copy-start.1
  0.7 0.0 copy-start.2
  0.7 0.0 copy-start.3
  0.7 0.0 copy-start.4
  0.7 18.9 %section.1 = (f32[5,5,5,2,128]{4,3,2,1,0:T(2,128)S(1)}, bf16[4,8,16,128]{3,2,1,0:T(8,128)(2,1)S(1)}, bf16[4,8,16,128]{3,2,1,0:T(8,128)(2,1)S(1)}) custom-call(f32[5,5,5,2,128]{4,3,2,1,0:T(2,128)} %bitcast.8, f32[3,5,5,5,2,128]{5,4,3,2,1,0:T(2,128)} %bitcast.7, s32[1,128]{1,0:T(1,128)} %bitcast.9, s32[1,128]{1,0:T(1,128)} %bitcast.10, ...), custom_call_target="tpu_custom_call" | custom-call | tf_op jit(solution)/shard_map/section/pallas_call | solution.py:469
  19.6 0.0 copy-done
  19.6 0.0 copy-done.1
  19.7 0.0 copy-done.2
  19.7 0.0 copy-done.3
  19.7 0.0 copy-done.4
  19.7 2.2 %train.1 = (f32[5,5,5,2,128]{4,3,2,1,0:T(2,128)}, f32[1,128,256]{2,1,0:T(8,128)}, f32[1,256,256]{2,1,0:T(8,128)}, f32[1,256,256]{2,1,0:T(8,128)}, f32[1,256,256]{2,1,0:T(8,128)}, /*index=5*/f32[1,256,128]{2,1,0:T(8,128)}) custom-call(f32[5,5,5,2,128]{4,3,2,1,0:T(2,128)S(1)} %get-tuple-element.15.new_ref, ...), custom_call_target="tpu_custom_call" | custom-call | tf_op jit(solution)/shard_map/train/pallas_call | solution.py:516
Async XLA Ops:
  0.6 19.0 %copy-start = (bf16[1,256,256]{2,1,0:T(8,128)(2,1)S(1)}, bf16[1,256,256]{2,1,0:T(8,128)(2,1)}, u32[]{:S(2)}) copy-start(bf16[1,256,256]{2,1,0:T(8,128)(2,1)} %two.1) | copy-start | bytes 393220
  0.6 19.0 %copy-start.1 = (bf16[1,256,256]{2,1,0:T(8,128)(2,1)S(1)}, bf16[1,256,256]{2,1,0:T(8,128)(2,1)}, u32[]{:S(2)}) copy-start(bf16[1,256,256]{2,1,0:T(8,128)(2,1)} %three.1) | copy-start | bytes 393220
  0.7 19.0 %copy-start.2 = (bf16[1,256,256]{2,1,0:T(8,128)(2,1)S(1)}, bf16[1,256,256]{2,1,0:T(8,128)(2,1)}, u32[]{:S(2)}) copy-start(bf16[1,256,256]{2,1,0:T(8,128)(2,1)} %four.1) | copy-start | bytes 393220
  0.7 19.0 %copy-start.3 = (bf16[1,128,256]{2,1,0:T(8,128)(2,1)S(1)}, bf16[1,128,256]{2,1,0:T(8,128)(2,1)}, u32[]{:S(2)}) copy-start(bf16[1,128,256]{2,1,0:T(8,128)(2,1)} %one.1) | copy-start | bytes 196612
  0.7 19.0 %copy-start.4 = (bf16[1,256,128]{2,1,0:T(8,128)(2,1)S(1)}, bf16[1,256,128]{2,1,0:T(8,128)(2,1)}, u32[]{:S(2)}) copy-start(bf16[1,256,128]{2,1,0:T(8,128)(2,1)} %five.1) | copy-start | bytes 196612

commit v4 on v3

--- a/solution.py
+++ b/solution.py
@@ -11,6 +11,7 @@
 
 P_SIZE = 5
 CAP = 16
+COPIES = 1
 MESH = pl.DeviceIdType.MESH
 
 
@@ -87,15 +88,45 @@
     return inner, left_value, right_value, edge_left, edge_right
 
 
-INNER, LEFT, RIGHT, EDGE_LEFT, EDGE_RIGHT = fr_tables()
-RANGE = range(P_SIZE)
-
-
-def weighted(table, parts):
-    total = parts[0] * np.float32(table[0])
-    for weight, part in zip(table[1:], parts[1:]):
-        total = total + part * np.float32(weight)
-    return total
+POINTS = P_SIZE**3
+FACES = 32
+
+
+def section_tables():
+    inner, left, right, edge_left, edge_right = fr_tables()
+    to_faces = np.zeros((3, 2, FACES, 128))
+    volume = np.zeros((128, 3, 128))
+    edges = np.zeros((128, 3, 2, FACES))
+    for point in range(POINTS):
+        place = (point // 25, point // 5 % 5, point % 5)
+        for d in range(3):
+            rest = [place[n] for n in range(3) if n != d]
+            face = rest[0] * P_SIZE + rest[1]
+            to_faces[d, 0, face, point] = left[place[d]]
+            to_faces[d, 1, face, point] = right[place[d]]
+            edges[point, d, 0, face] = edge_left[place[d]]
+            edges[point, d, 1, face] = edge_right[place[d]]
+            for m in range(P_SIZE):
+                source = point + (m - place[d]) * (25, 5, 1)[d]
+                volume[point, d, source] = inner[place[d]][m]
+
+    def halves(table):
+        high = table.astype(np.float32).astype(jnp.bfloat16)
+        low = (table - high.astype(np.float64)).astype(np.float32).astype(jnp.bfloat16)
+        return np.stack([high, low])
+
+    second = np.concatenate([volume.reshape(128, -1), edges.reshape(128, -1)], axis=1)
+    return halves(to_faces.reshape(-1, 128)), halves(second)
+
+
+FACE_TABLE, POINT_TABLE = section_tables()
+
+
+def apply(table, x):
+    high = x.astype(jnp.bfloat16)
+    low = (x - high.astype(jnp.float32)).astype(jnp.bfloat16)
+    dot = functools.partial(jnp.dot, preferred_element_type=jnp.float32)
+    return dot(table[0], high) + (dot(table[0], low) + dot(table[1], high))
 
 
 def upwind(state_before, speed_before, state_after, speed_after):
@@ -103,9 +134,9 @@
     return speed * (state_before + state_after) - jnp.abs(speed) * (state_after - state_before)
 
 
-def beside(x, y, row, other=None):
-    other = row if other is None else other
-    return jnp.concatenate([x[..., row : row + 1, :], y[..., other : other + 1, :]], axis=-2)
+def turn(x, step):
+    half = x.shape[1] // 2
+    return jnp.concatenate([pltpu.roll(x[:, :half], step % half, 1), pltpu.roll(x[:, half:], step % half, 1)], axis=1)
 
 
 def paired(place, d):
@@ -121,17 +152,13 @@
     return spans * CAP == samples
 
 
-def shift(x, step):
-    return jnp.concatenate([x[..., -step:], x[..., :-step]], axis=-1)
-
-
 def section_kernel(
     spans, walls,
-    field_hbm, velocity_hbm, cells_hbm, dest_hbm, targets_hbm,
+    field_hbm, velocity_hbm, cells_hbm, dest_hbm, targets_hbm, face_hbm, point_hbm,
     new_ref, rows_all, marks_all,
-    field, velocity, cells_ref, dest_ref, targets_ref,
-    own_zero, own_one, one_send, zero_before, zero_after, one_before, one_after,
-    flat, rows_send, marks_send,
+    field, velocity, cells_ref, dest_ref, targets_ref, face_table, point_table,
+    zero_send, one_send, zero_before, zero_after, one_before, one_after,
+    values, rows_send, marks_send,
     in_sems, halo_send, halo_recv,
     marks_sems, marks_wall_sems, rows_sems, rows_wall_sems,
 ):
@@ -143,11 +170,19 @@
     for d in range(1, walls):
         pl.semaphore_signal(barrier, inc=1, device_id={"wall": lax.rem(w + d, walls)}, device_id_type=MESH)
 
-    loads = [pltpu.make_async_copy(field_hbm, field, in_sems.at[0])]
+    flat = 2 * POINTS
+    loads = [
+        pltpu.make_async_copy(field_hbm.reshape(flat, 128), field.at[0:flat], in_sems.at[0]),
+        pltpu.make_async_copy(face_hbm, face_table, in_sems.at[1]),
+    ]
     for d in range(3):
-        loads.append(pltpu.make_async_copy(velocity_hbm.at[d], velocity.at[d], in_sems.at[1 + d]))
-    for number, (whole, ref) in enumerate(((dest_hbm, dest_ref), (targets_hbm, targets_ref), (cells_hbm, cells_ref))):
-        loads.append(pltpu.make_async_copy(whole, ref, in_sems.at[4 + number]))
+        loads.append(
+            pltpu.make_async_copy(velocity_hbm.at[d].reshape(flat, 128), velocity.at[d, 0:flat], in_sems.at[2 + d])
+        )
+    for number, (whole, ref) in enumerate(
+        ((dest_hbm, dest_ref), (targets_hbm, targets_ref), (cells_hbm, cells_ref), (point_hbm, point_table))
+    ):
+        loads.append(pltpu.make_async_copy(whole, ref, in_sems.at[5 + number]))
     for load in loads:
         load.start()
 
@@ -156,25 +191,27 @@
         def _(ref=ref):
             ref[...] = jnp.zeros_like(ref)
 
+    field[flat:] = jnp.zeros((256 - flat, 128), jnp.float32)
+    velocity[:, flat:] = jnp.zeros((3, 256 - flat, 128), jnp.float32)
+
+    def beside(ref, *at):
+        return jnp.concatenate([ref[at + (pl.ds(b, 128, stride=2),)] for b in range(2)], axis=1)
+
     loads[0].wait()
     loads[1].wait()
-    for j in RANGE:
-        q = [field[m, j] for m in RANGE]
-        a = [velocity[0, m, j] for m in RANGE]
-        own_zero[0, j] = weighted(LEFT, q)
-        own_zero[1, j] = weighted(LEFT, a)
-        own_zero[2, j] = weighted(RIGHT, q)
-        own_zero[3, j] = weighted(RIGHT, a)
+    two = 2 * FACES
+    q = beside(field)
+    face_q = apply(face_table[:, 0 : 2 * two], q)
+    q_zero, q_one = face_q[:two], face_q[two:]
     loads[2].wait()
-    for m0 in RANGE:
-        q = [field[m0, m] for m in RANGE]
-        a = [velocity[1, m0, m] for m in RANGE]
-        own_one[0, m0] = weighted(LEFT, q)
-        own_one[1, m0] = weighted(LEFT, a)
-        own_one[2, m0] = weighted(RIGHT, q)
-        own_one[3, m0] = weighted(RIGHT, a)
-        one_send[0, m0] = beside(own_one[0, m0], own_one[1, m0], 0)
-        one_send[1, m0] = beside(own_one[2, m0], own_one[3, m0], 1)
+    a_zero = apply(face_table[:, 0:two], beside(velocity, 0))
+    loads[3].wait()
+    a_one = apply(face_table[:, two : 2 * two], beside(velocity, 1))
+    for n, (along_zero, along_one) in enumerate(((q_zero, q_one), (a_zero, a_one))):
+        zero_send[0, n] = along_zero[:FACES]
+        zero_send[1, n] = along_zero[FACES:]
+        one_send[0, n] = along_one[:FACES, :128]
+        one_send[1, n] = along_one[FACES:, 128:]
 
     pl.semaphore_wait(barrier, spans + walls - 2)
 
@@ -193,8 +230,8 @@
         return copy, sends, gets
 
     halos = [
-        halo(0, "span", i, spans, own_zero.at[2:4], zero_before, True),
-        halo(1, "span", i, spans, own_zero.at[0:2], zero_after, False),
+        halo(0, "span", i, spans, zero_send.at[1], zero_before, True),
+        halo(1, "span", i, spans, zero_send.at[0], zero_after, False),
         halo(2, "wall", w, walls, one_send.at[1], one_before, True),
         halo(3, "wall", w, walls, one_send.at[0], one_after, False),
     ]
@@ -202,7 +239,7 @@
         pl.when(sends)(copy.start)
 
     samples = dest_ref.shape[1]
-    for load in loads[4:]:
+    for load in loads[5:8]:
         load.wait()
     dest = dest_ref[...]
     across = jnp.broadcast_to(dest, (samples, samples))
@@ -220,7 +257,7 @@
         flags = jnp.dot(chosen, jnp.ones((samples, samples), jnp.bfloat16), preferred_element_type=jnp.float32)
         marks_send[:, CAP : 2 * CAP] = flags.astype(jnp.bfloat16).reshape(spans, CAP, -1)
 
-    groups = min(spans, 8)
+    groups = min(spans, COPIES)
     size = spans // groups
 
     def group_of(held, wall, g):
@@ -294,86 +331,50 @@
     sent = dispatch(marks_send, marks_all, marks_sems, marks_wall_sems)
 
     cells = cells_ref[...]
-    picks = []
-    for b in range(2):
-        here = jnp.where(
-            lax.broadcasted_iota(jnp.int32, (samples, samples), 0) + b * samples == cells, 1.0, 0.0
-        ).astype(jnp.bfloat16)
-        pick = lax.dot_general(
-            chosen, here, (((1,), (1,)), ((), ())), preferred_element_type=jnp.float32
-        )
-        picks.append(pick.astype(jnp.bfloat16))
-
-    loads[3].wait()
-    means = [0.0, 0.0, 0.0]
-    for m0 in RANGE:
-        q = [field[m0, :, m] for m in RANGE]
-        a = [velocity[2, m0, :, m] for m in RANGE]
-        means[2] = means[2] + jnp.sum(a[0] + a[1] + a[2] + a[3] + a[4], axis=0)
-        q_left, a_left, q_right, a_right = (
-            weighted(LEFT, q), weighted(LEFT, a), weighted(RIGHT, q), weighted(RIGHT, a)
-        )
-        left = upwind(shift(q_right, 1), shift(a_right, 1), q_left, a_left)
-        right = upwind(q_right, a_right, shift(q_left, -1), shift(a_left, -1))
-        f = [x * y for x, y in zip(q, a)]
-        for k in RANGE:
-            new_ref[m0, :, k] = q[k] - (
-                weighted(INNER[k], f)
-                + left * np.float32(EDGE_LEFT[k])
-                + right * np.float32(EDGE_RIGHT[k])
-            )
-    for m0 in RANGE:
-        a = [velocity[1, m0, m] for m in RANGE]
-        means[1] = means[1] + jnp.sum(a[0] + a[1] + a[2] + a[3] + a[4], axis=0)
-        f = [field[m0, m] * a[m] for m in RANGE]
-        for k in RANGE:
-            new_ref[m0, k] = new_ref[m0, k] - weighted(INNER[k], f)
-    for j in RANGE:
-        a = [velocity[0, m, j] for m in RANGE]
-        means[0] = means[0] + jnp.sum(a[0] + a[1] + a[2] + a[3] + a[4], axis=0)
-        f = [field[m, j] * a[m] for m in RANGE]
-        for k in RANGE:
-            new_ref[k, j] = new_ref[k, j] - weighted(INNER[k], f)
-    points = P_SIZE**3
+    here = jnp.where(
+        lax.broadcasted_iota(jnp.int32, (2 * samples, samples), 0) == cells, 1.0, 0.0
+    ).astype(jnp.bfloat16)
+    picks = lax.dot_general(
+        chosen, here, (((1,), (1,)), ((), ())), preferred_element_type=jnp.float32
+    ).astype(jnp.bfloat16)
+
+    loads[4].wait()
+    loads[8].wait()
+    a = [beside(velocity, d) for d in range(3)]
+    q_two = apply(face_table[:, 2 * two :], q)
+    a_two = apply(face_table[:, 2 * two :], a[2])
+    left = upwind(turn(q_two[FACES:], 1), turn(a_two[FACES:], 1), q_two[:FACES], a_two[:FACES])
+    right = upwind(q_two[FACES:], a_two[FACES:], turn(q_two[:FACES], -1), turn(a_two[:FACES], -1))
+    edges = 3 * 128
+    partial = q - (
+        apply(point_table[:, :, :edges], jnp.concatenate([q * x for x in a], axis=0))
+        + apply(point_table[:, :, edges + 2 * two :], jnp.concatenate([left, right], axis=0))
+    )
+    means = [jnp.sum(x, axis=0, keepdims=True) * np.float32(1.0 / POINTS) for x in a]
+
+    sent += pass_on(marks_all, marks_sems, marks_wall_sems)
+
+    for copy, _, gets in halos:
+        pl.when(gets)(copy.wait_recv)
+    shared = [
+        upwind(zero_before[0], zero_before[1], q_zero[:FACES], a_zero[:FACES]),
+        upwind(q_zero[FACES:], a_zero[FACES:], zero_after[0], zero_after[1]),
+    ]
+    before = [jnp.concatenate([one_before[n], x[FACES:, :128]], axis=1) for n, x in enumerate((q_one, a_one))]
+    after = [jnp.concatenate([x[:FACES, 128:], one_after[n]], axis=1) for n, x in enumerate((q_one, a_one))]
+    shared.append(upwind(before[0], before[1], q_one[:FACES], a_one[:FACES]))
+    shared.append(upwind(q_one[FACES:], a_one[FACES:], after[0], after[1]))
+    new = partial - apply(point_table[:, :, edges : edges + 2 * two], jnp.concatenate(shared, axis=0))
+    values[...] = new
     for d in range(3):
-        flat[2 * (points + d) : 2 * (points + d) + 2] = means[d] * np.float32(1.0 / points)
-
-    sent += pass_on(marks_all, marks_sems, marks_wall_sems)
-
-    for copy, _, gets in halos[:2]:
-        pl.when(gets)(copy.wait_recv)
-    for j in RANGE:
-        left = upwind(zero_before[0, j], zero_before[1, j], own_zero[0, j], own_zero[1, j])
-        right = upwind(own_zero[2, j], own_zero[3, j], zero_after[0, j], zero_after[1, j])
-        for k in RANGE:
-            new_ref[k, j] = new_ref[k, j] - (
-                left * np.float32(EDGE_LEFT[k]) + right * np.float32(EDGE_RIGHT[k])
-            )
-    for copy, _, gets in halos[2:]:
-        pl.when(gets)(copy.wait_recv)
-    for m0 in RANGE:
-        before = [beside(one_before[m0], own_one[2 + n, m0], n, 0) for n in range(2)]
-        after = [beside(own_one[n, m0], one_after[m0], 1, n) for n in range(2)]
-        left = upwind(before[0], before[1], own_one[0, m0], own_one[1, m0])
-        right = upwind(own_one[2, m0], own_one[3, m0], after[0], after[1])
-        for k in RANGE:
-            value = new_ref[m0, k] - (
-                left * np.float32(EDGE_LEFT[k]) + right * np.float32(EDGE_RIGHT[k])
-            )
-            new_ref[m0, k] = value
-            for n in RANGE:
-                point = (m0 * P_SIZE + k) * P_SIZE + n
-                flat[2 * point : 2 * point + 2] = value[n]
-
-    total = None
-    for b in range(2):
-        values = flat[pl.ds(b, points + 3, stride=2)].astype(jnp.bfloat16)
-        part = lax.dot_general(
-            picks[b], values, (((1,), (1,)), ((), ())), preferred_element_type=jnp.float32
-        )
-        total = part if total is None else total + part
+        values[POINTS + d : POINTS + d + 1] = means[d]
+    total = lax.dot_general(
+        picks, values[...].astype(jnp.bfloat16), (((1,), (1,)), ((), ())), preferred_element_type=jnp.float32
+    )
     rows_send[...] = total.astype(jnp.bfloat16).reshape(rows_send.shape)
     sent += dispatch(rows_send, rows_all, rows_sems, rows_wall_sems)
+    for b in range(2):
+        new_ref.reshape(flat, 128)[pl.ds(b, POINTS, stride=2)] = new[:POINTS, b * 128 : (b + 1) * 128]
     sent += pass_on(rows_all, rows_sems, rows_wall_sems)
     for copy, sends, _ in halos:
         pl.when(sends)(copy.wait_send)
@@ -457,7 +458,6 @@
     shape = field.shape
     samples = cells.shape[0]
     inside = (P_SIZE, P_SIZE, P_SIZE, shape[3] * shape[4], shape[5])
-    faces = (P_SIZE, P_SIZE) + inside[3:]
     vmem = pl.BlockSpec(memory_space=pltpu.VMEM)
     anywhere = pl.BlockSpec(memory_space=pl.ANY)
     hbm = pl.BlockSpec(memory_space=pltpu.HBM)
@@ -473,26 +473,27 @@
             jax.ShapeDtypeStruct((walls, spans, CAP, features), jnp.bfloat16),
             jax.ShapeDtypeStruct((walls, spans, marks, wide), jnp.bfloat16),
         ),
-        in_specs=[hbm] * 5,
+        in_specs=[hbm] * 7,
         out_specs=(vmem,) * 3,
         scratch_shapes=[
-            pltpu.VMEM(inside, jnp.float32),
-            pltpu.VMEM((3,) + inside, jnp.float32),
+            pltpu.VMEM((256, 128), jnp.float32),
+            pltpu.VMEM((3, 256, 128), jnp.float32),
             pltpu.VMEM((1, samples), jnp.int32),
             pltpu.VMEM((1, samples), jnp.int32),
             pltpu.VMEM(targets.shape, jnp.bfloat16),
-            pltpu.VMEM((4,) + faces, jnp.float32),
-            pltpu.VMEM((4,) + faces, jnp.float32),
-            pltpu.VMEM((2,) + faces, jnp.float32),
-            pltpu.VMEM((2,) + faces, jnp.float32),
-            pltpu.VMEM((2,) + faces, jnp.float32),
-            pltpu.VMEM(faces, jnp.float32),
-            pltpu.VMEM(faces, jnp.float32),
-            pltpu.VMEM((2 * features, shape[5]), jnp.float32),
+            pltpu.VMEM(FACE_TABLE.shape, jnp.bfloat16),
+            pltpu.VMEM(POINT_TABLE.shape, jnp.bfloat16),
+            pltpu.VMEM((2, 2, FACES, 256), jnp.float32),
+            pltpu.VMEM((2, 2, FACES, 128), jnp.float32),
+            pltpu.VMEM((2, FACES, 256), jnp.float32),
+            pltpu.VMEM((2, FACES, 256), jnp.float32),
+            pltpu.VMEM((2, FACES, 128), jnp.float32),
+            pltpu.VMEM((2, FACES, 128), jnp.float32),
+            pltpu.VMEM((128, 256), jnp.float32),
             pltpu.VMEM((spans, CAP, features), jnp.bfloat16),
             pltpu.VMEM((spans, marks, wide), jnp.bfloat16),
-            dma((7,)), dma((4,)), dma((4,)),
-            dma((2, spans)), dma((2, walls, min(spans, 8))), dma((2, spans)), dma((2, walls, min(spans, 8))),
+            dma((9,)), dma((4,)), dma((4,)),
+            dma((2, spans)), dma((2, walls, min(spans, COPIES))), dma((2, spans)), dma((2, walls, min(spans, COPIES))),
         ],
         compiler_params=pltpu.CompilerParams(
             collective_id=0, has_side_effects=True, vmem_limit_bytes=48 * 1024 * 1024
@@ -507,6 +508,8 @@
                 cells.reshape(1, samples),
                 destination.reshape(1, samples),
                 targets,
+                jnp.asarray(FACE_TABLE),
+                jnp.asarray(POINT_TABLE),
             )
         )
     )

time: 22.1 us -> 21.8 us (0.986)
  Pallas kernels: 21.2 us -> 20.9 us
    pallas_call x1, Pallas kernels: 18.9 us -> 18.7 us  [local(): pl.pallas_call(functools.partial(section_kernel, spans, walls), out_shape...]
where the time goes in v4:
time: 21.8 us; the launch traced here: 21.6 us
  Pallas kernels  20.9 us (96%)
  between operations  0.72 us (3%)
    pallas_call x1, Pallas kernels, local(): pl.pallas_call(functools.partial(section_kernel, spans, walls), out_shape...  18.7 us
    pallas_call x1, Pallas kernels, local(): pl.pallas_call(functools.partial(train_kernel, per_chunk, full), out_shap...  2.21 us

profile of v4, /device:TPU:0, one launch (start us, length us, event | category | flops | bytes accessed | tf_op | source)
XLA Modules:
  0.0 21.6 jit_solution(13809557010408256312)
XLA Ops:
  0.6 0.0 copy-start
  0.6 0.0 copy-start.1
  0.7 0.0 copy-start.2
  0.7 0.0 copy-start.3
  0.7 0.0 copy-start.4
  0.7 18.7 %section.1 = (f32[5,5,5,2,128]{4,3,2,1,0:T(2,128)S(1)}, bf16[4,8,16,128]{3,2,1,0:T(8,128)(2,1)S(1)}, bf16[4,8,16,128]{3,2,1,0:T(8,128)(2,1)S(1)}) custom-call(f32[5,5,5,2,128]{4,3,2,1,0:T(2,128)} %bitcast.8, f32[3,5,5,5,2,128]{5,4,3,2,1,0:T(2,128)} %bitcast.7, s32[1,128]{1,0:T(1,128)} %bitcast.9, s32[1,128]{1,0:T(1,128)} %bitcast.10, ...), custom_call_target="tpu_custom_call" | custom-call | tf_op jit(solution)/shard_map/section/pallas_call | solution.py:469
  19.4 0.0 copy-done
  19.4 0.0 copy-done.1
  19.4 0.0 copy-done.2
  19.4 0.0 copy-done.3
  19.4 0.0 copy-done.4
  19.4 2.2 %train.1 = (f32[5,5,5,2,128]{4,3,2,1,0:T(2,128)}, f32[1,128,256]{2,1,0:T(8,128)}, f32[1,256,256]{2,1,0:T(8,128)}, f32[1,256,256]{2,1,0:T(8,128)}, f32[1,256,256]{2,1,0:T(8,128)}, /*index=5*/f32[1,256,128]{2,1,0:T(8,128)}) custom-call(f32[5,5,5,2,128]{4,3,2,1,0:T(2,128)S(1)} %get-tuple-element.15.new_ref, ...), custom_call_target="tpu_custom_call" | custom-call | tf_op jit(solution)/shard_map/train/pallas_call | solution.py:519
Async XLA Ops:
  0.6 18.7 %copy-start = (bf16[1,256,256]{2,1,0:T(8,128)(2,1)S(1)}, bf16[1,256,256]{2,1,0:T(8,128)(2,1)}, u32[]{:S(2)}) copy-start(bf16[1,256,256]{2,1,0:T(8,128)(2,1)} %two.1) | copy-start | bytes 393220
  0.6 18.7 %copy-start.1 = (bf16[1,256,256]{2,1,0:T(8,128)(2,1)S(1)}, bf16[1,256,256]{2,1,0:T(8,128)(2,1)}, u32[]{:S(2)}) copy-start(bf16[1,256,256]{2,1,0:T(8,128)(2,1)} %three.1) | copy-start | bytes 393220
  0.7 18.7 %copy-start.2 = (bf16[1,256,256]{2,1,0:T(8,128)(2,1)S(1)}, bf16[1,256,256]{2,1,0:T(8,128)(2,1)}, u32[]{:S(2)}) copy-start(bf16[1,256,256]{2,1,0:T(8,128)(2,1)} %four.1) | copy-start | bytes 393220
  0.7 18.7 %copy-start.3 = (bf16[1,128,256]{2,1,0:T(8,128)(2,1)S(1)}, bf16[1,128,256]{2,1,0:T(8,128)(2,1)}, u32[]{:S(2)}) copy-start(bf16[1,128,256]{2,1,0:T(8,128)(2,1)} %one.1) | copy-start | bytes 196612
  0.7 18.7 %copy-start.4 = (bf16[1,256,128]{2,1,0:T(8,128)(2,1)S(1)}, bf16[1,256,128]{2,1,0:T(8,128)(2,1)}, u32[]{:S(2)}) copy-start(bf16[1,256,128]{2,1,0:T(8,128)(2,1)} %five.1) | copy-start | bytes 196612

commit v5 on v4

--- a/solution.py
+++ b/solution.py
@@ -165,10 +165,10 @@
     i = lax.axis_index("span")
     w = lax.axis_index("wall")
     barrier = pltpu.get_barrier_semaphore()
-    for d in range(1, spans):
-        pl.semaphore_signal(barrier, inc=1, device_id={"span": lax.rem(i + d, spans)}, device_id_type=MESH)
-    for d in range(1, walls):
-        pl.semaphore_signal(barrier, inc=1, device_id={"wall": lax.rem(w + d, walls)}, device_id_type=MESH)
+    for d in reversed(range(1, spans)):
+        pl.semaphore_signal(barrier, inc=1, device_id={"span": paired(i, d)}, device_id_type=MESH)
+    for d in reversed(range(1, walls)):
+        pl.semaphore_signal(barrier, inc=1, device_id={"wall": paired(w, d)}, device_id_type=MESH)
 
     flat = 2 * POINTS
     loads = [
@@ -208,10 +208,10 @@
     loads[3].wait()
     a_one = apply(face_table[:, two : 2 * two], beside(velocity, 1))
     for n, (along_zero, along_one) in enumerate(((q_zero, q_one), (a_zero, a_one))):
-        zero_send[0, n] = along_zero[:FACES]
-        zero_send[1, n] = along_zero[FACES:]
-        one_send[0, n] = along_one[:FACES, :128]
-        one_send[1, n] = along_one[FACES:, 128:]
+        zero_send[0, n] = along_zero[:FACES].astype(jnp.bfloat16)
+        zero_send[1, n] = along_zero[FACES:].astype(jnp.bfloat16)
+        one_send[0, n] = along_one[:FACES, :128].astype(jnp.bfloat16)
+        one_send[1, n] = along_one[FACES:, 128:].astype(jnp.bfloat16)
 
     pl.semaphore_wait(barrier, spans + walls - 2)
 
@@ -273,7 +273,7 @@
                 device_id={"span": paired(i, d)},
                 device_id_type=MESH,
             )
-            for d in range(1, spans)
+            for d in reversed(range(1, spans))
         ]
         for copy in copies:
             copy.start()
@@ -293,7 +293,7 @@
                 device_id={"wall": paired(w, n)},
                 device_id_type=MESH,
             )
-            for n in range(1, walls)
+            for n in reversed(range(1, walls))
         ]
         for copy in copies:
             copy.start()
@@ -356,12 +356,13 @@
 
     for copy, _, gets in halos:
         pl.when(gets)(copy.wait_recv)
+    got = [[ref[n].astype(jnp.float32) for n in range(2)] for ref in (zero_before, zero_after, one_before, one_after)]
     shared = [
-        upwind(zero_before[0], zero_before[1], q_zero[:FACES], a_zero[:FACES]),
-        upwind(q_zero[FACES:], a_zero[FACES:], zero_after[0], zero_after[1]),
+        upwind(*got[0], q_zero[:FACES], a_zero[:FACES]),
+        upwind(q_zero[FACES:], a_zero[FACES:], *got[1]),
     ]
-    before = [jnp.concatenate([one_before[n], x[FACES:, :128]], axis=1) for n, x in enumerate((q_one, a_one))]
-    after = [jnp.concatenate([x[:FACES, 128:], one_after[n]], axis=1) for n, x in enumerate((q_one, a_one))]
+    before = [jnp.concatenate([got[2][n], x[FACES:, :128]], axis=1) for n, x in enumerate((q_one, a_one))]
+    after = [jnp.concatenate([x[:FACES, 128:], got[3][n]], axis=1) for n, x in enumerate((q_one, a_one))]
     shared.append(upwind(before[0], before[1], q_one[:FACES], a_one[:FACES]))
     shared.append(upwind(q_one[FACES:], a_one[FACES:], after[0], after[1]))
     new = partial - apply(point_table[:, :, edges : edges + 2 * two], jnp.concatenate(shared, axis=0))
@@ -483,12 +484,12 @@
             pltpu.VMEM(targets.shape, jnp.bfloat16),
             pltpu.VMEM(FACE_TABLE.shape, jnp.bfloat16),
             pltpu.VMEM(POINT_TABLE.shape, jnp.bfloat16),
-            pltpu.VMEM((2, 2, FACES, 256), jnp.float32),
-            pltpu.VMEM((2, 2, FACES, 128), jnp.float32),
-            pltpu.VMEM((2, FACES, 256), jnp.float32),
-            pltpu.VMEM((2, FACES, 256), jnp.float32),
-            pltpu.VMEM((2, FACES, 128), jnp.float32),
-            pltpu.VMEM((2, FACES, 128), jnp.float32),
+            pltpu.VMEM((2, 2, FACES, 256), jnp.bfloat16),
+            pltpu.VMEM((2, 2, FACES, 128), jnp.bfloat16),
+            pltpu.VMEM((2, FACES, 256), jnp.bfloat16),
+            pltpu.VMEM((2, FACES, 256), jnp.bfloat16),
+            pltpu.VMEM((2, FACES, 128), jnp.bfloat16),
+            pltpu.VMEM((2, FACES, 128), jnp.bfloat16),
             pltpu.VMEM((128, 256), jnp.float32),
             pltpu.VMEM((spans, CAP, features), jnp.bfloat16),
             pltpu.VMEM((spans, marks, wide), jnp.bfloat16),

time: 21.8 us -> 20.9 us (0.959)
  Pallas kernels: 20.9 us -> 20 us
    pallas_call x1, Pallas kernels: 18.7 us -> 17.8 us  [local(): pl.pallas_call(functools.partial(section_kernel, spans, walls), out_shape...]
where the time goes in v5:
time: 20.9 us; the launch traced here: 20.8 us
  Pallas kernels  20 us (96%)
  between operations  0.72 us (3%)
    pallas_call x1, Pallas kernels, local(): pl.pallas_call(functools.partial(section_kernel, spans, walls), out_shape...  17.8 us
    pallas_call x1, Pallas kernels, local(): pl.pallas_call(functools.partial(train_kernel, per_chunk, full), out_shap...  2.21 us

profile of v5, /device:TPU:0, one launch (start us, length us, event | category | flops | bytes accessed | tf_op | source)
XLA Modules:
  0.0 20.8 jit_solution(13009632137018179650)
XLA Ops:
  0.6 0.0 copy-start
  0.6 0.0 copy-start.1
  0.7 0.0 copy-start.2
  0.7 0.0 copy-start.3
  0.7 0.0 copy-start.4
  0.7 17.8 %section.1 = (f32[5,5,5,2,128]{4,3,2,1,0:T(2,128)S(1)}, bf16[4,8,16,128]{3,2,1,0:T(8,128)(2,1)S(1)}, bf16[4,8,16,128]{3,2,1,0:T(8,128)(2,1)S(1)}) custom-call(f32[5,5,5,2,128]{4,3,2,1,0:T(2,128)} %bitcast.8, f32[3,5,5,5,2,128]{5,4,3,2,1,0:T(2,128)} %bitcast.7, s32[1,128]{1,0:T(1,128)} %bitcast.9, s32[1,128]{1,0:T(1,128)} %bitcast.10, ...), custom_call_target="tpu_custom_call" | custom-call | tf_op jit(solution)/shard_map/section/pallas_call | solution.py:470
  18.5 0.0 copy-done
  18.5 0.0 copy-done.1
  18.5 0.0 copy-done.2
  18.5 0.0 copy-done.3
  18.5 0.0 copy-done.4
  18.5 2.2 %train.1 = (f32[5,5,5,2,128]{4,3,2,1,0:T(2,128)}, f32[1,128,256]{2,1,0:T(8,128)}, f32[1,256,256]{2,1,0:T(8,128)}, f32[1,256,256]{2,1,0:T(8,128)}, f32[1,256,256]{2,1,0:T(8,128)}, /*index=5*/f32[1,256,128]{2,1,0:T(8,128)}) custom-call(f32[5,5,5,2,128]{4,3,2,1,0:T(2,128)S(1)} %get-tuple-element.15.new_ref, ...), custom_call_target="tpu_custom_call" | custom-call | tf_op jit(solution)/shard_map/train/pallas_call | solution.py:520
Async XLA Ops:
  0.6 17.9 %copy-start = (bf16[1,256,256]{2,1,0:T(8,128)(2,1)S(1)}, bf16[1,256,256]{2,1,0:T(8,128)(2,1)}, u32[]{:S(2)}) copy-start(bf16[1,256,256]{2,1,0:T(8,128)(2,1)} %two.1) | copy-start | bytes 393220
  0.6 17.9 %copy-start.1 = (bf16[1,256,256]{2,1,0:T(8,128)(2,1)S(1)}, bf16[1,256,256]{2,1,0:T(8,128)(2,1)}, u32[]{:S(2)}) copy-start(bf16[1,256,256]{2,1,0:T(8,128)(2,1)} %three.1) | copy-start | bytes 393220
  0.7 17.9 %copy-start.2 = (bf16[1,256,256]{2,1,0:T(8,128)(2,1)S(1)}, bf16[1,256,256]{2,1,0:T(8,128)(2,1)}, u32[]{:S(2)}) copy-start(bf16[1,256,256]{2,1,0:T(8,128)(2,1)} %four.1) | copy-start | bytes 393220
  0.7 17.9 %copy-start.3 = (bf16[1,128,256]{2,1,0:T(8,128)(2,1)S(1)}, bf16[1,128,256]{2,1,0:T(8,128)(2,1)}, u32[]{:S(2)}) copy-start(bf16[1,128,256]{2,1,0:T(8,128)(2,1)} %one.1) | copy-start | bytes 196612
  0.7 17.9 %copy-start.4 = (bf16[1,256,128]{2,1,0:T(8,128)(2,1)S(1)}, bf16[1,256,128]{2,1,0:T(8,128)(2,1)}, u32[]{:S(2)}) copy-start(bf16[1,256,128]{2,1,0:T(8,128)(2,1)} %five.1) | copy-start | bytes 196612

commit v6 on v4

--- a/solution.py
+++ b/solution.py
@@ -125,8 +125,11 @@
 def apply(table, x):
     high = x.astype(jnp.bfloat16)
     low = (x - high.astype(jnp.float32)).astype(jnp.bfloat16)
-    dot = functools.partial(jnp.dot, preferred_element_type=jnp.float32)
-    return dot(table[0], high) + (dot(table[0], low) + dot(table[1], high))
+    return jnp.dot(
+        jnp.concatenate([table[0], table[0], table[1]], axis=1),
+        jnp.concatenate([high, low, high], axis=0),
+        preferred_element_type=jnp.float32,
+    )
 
 
 def upwind(state_before, speed_before, state_after, speed_after):
@@ -158,17 +161,17 @@
     new_ref, rows_all, marks_all,
     field, velocity, cells_ref, dest_ref, targets_ref, face_table, point_table,
     zero_send, one_send, zero_before, zero_after, one_before, one_after,
-    values, rows_send, marks_send,
+    rows_send, marks_send,
     in_sems, halo_send, halo_recv,
     marks_sems, marks_wall_sems, rows_sems, rows_wall_sems,
 ):
     i = lax.axis_index("span")
     w = lax.axis_index("wall")
     barrier = pltpu.get_barrier_semaphore()
-    for d in range(1, spans):
-        pl.semaphore_signal(barrier, inc=1, device_id={"span": lax.rem(i + d, spans)}, device_id_type=MESH)
-    for d in range(1, walls):
-        pl.semaphore_signal(barrier, inc=1, device_id={"wall": lax.rem(w + d, walls)}, device_id_type=MESH)
+    for d in reversed(range(1, spans)):
+        pl.semaphore_signal(barrier, inc=1, device_id={"span": paired(i, d)}, device_id_type=MESH)
+    for d in reversed(range(1, walls)):
+        pl.semaphore_signal(barrier, inc=1, device_id={"wall": paired(w, d)}, device_id_type=MESH)
 
     flat = 2 * POINTS
     loads = [
@@ -230,10 +233,10 @@
         return copy, sends, gets
 
     halos = [
+        halo(2, "wall", w, walls, one_send.at[1], one_before, True),
+        halo(3, "wall", w, walls, one_send.at[0], one_after, False),
         halo(0, "span", i, spans, zero_send.at[1], zero_before, True),
         halo(1, "span", i, spans, zero_send.at[0], zero_after, False),
-        halo(2, "wall", w, walls, one_send.at[1], one_before, True),
-        halo(3, "wall", w, walls, one_send.at[0], one_after, False),
     ]
     for copy, sends, _ in halos:
         pl.when(sends)(copy.start)
@@ -273,7 +276,7 @@
                 device_id={"span": paired(i, d)},
                 device_id_type=MESH,
             )
-            for d in range(1, spans)
+            for d in reversed(range(1, spans))
         ]
         for copy in copies:
             copy.start()
@@ -293,7 +296,7 @@
                 device_id={"wall": paired(w, n)},
                 device_id_type=MESH,
             )
-            for n in range(1, walls)
+            for n in reversed(range(1, walls))
         ]
         for copy in copies:
             copy.start()
@@ -350,29 +353,30 @@
         apply(point_table[:, :, :edges], jnp.concatenate([q * x for x in a], axis=0))
         + apply(point_table[:, :, edges + 2 * two :], jnp.concatenate([left, right], axis=0))
     )
-    means = [jnp.sum(x, axis=0, keepdims=True) * np.float32(1.0 / POINTS) for x in a]
-
-    sent += pass_on(marks_all, marks_sems, marks_wall_sems)
+    row = lax.broadcasted_iota(jnp.int32, partial.shape, 0)
+    for d in range(3):
+        mean = jnp.sum(a[d], axis=0, keepdims=True) * np.float32(1.0 / POINTS)
+        partial = jnp.where(row == POINTS + d, mean, partial)
+
 
     for copy, _, gets in halos:
         pl.when(gets)(copy.wait_recv)
+    got = [[ref[n] for n in range(2)] for ref in (zero_before, zero_after, one_before, one_after)]
     shared = [
-        upwind(zero_before[0], zero_before[1], q_zero[:FACES], a_zero[:FACES]),
-        upwind(q_zero[FACES:], a_zero[FACES:], zero_after[0], zero_after[1]),
+        upwind(*got[0], q_zero[:FACES], a_zero[:FACES]),
+        upwind(q_zero[FACES:], a_zero[FACES:], *got[1]),
     ]
-    before = [jnp.concatenate([one_before[n], x[FACES:, :128]], axis=1) for n, x in enumerate((q_one, a_one))]
-    after = [jnp.concatenate([x[:FACES, 128:], one_after[n]], axis=1) for n, x in enumerate((q_one, a_one))]
+    before = [jnp.concatenate([got[2][n], x[FACES:, :128]], axis=1) for n, x in enumerate((q_one, a_one))]
+    after = [jnp.concatenate([x[:FACES, 128:], got[3][n]], axis=1) for n, x in enumerate((q_one, a_one))]
     shared.append(upwind(before[0], before[1], q_one[:FACES], a_one[:FACES]))
     shared.append(upwind(q_one[FACES:], a_one[FACES:], after[0], after[1]))
     new = partial - apply(point_table[:, :, edges : edges + 2 * two], jnp.concatenate(shared, axis=0))
-    values[...] = new
-    for d in range(3):
-        values[POINTS + d : POINTS + d + 1] = means[d]
     total = lax.dot_general(
-        picks, values[...].astype(jnp.bfloat16), (((1,), (1,)), ((), ())), preferred_element_type=jnp.float32
+        picks, new.astype(jnp.bfloat16), (((1,), (1,)), ((), ())), preferred_element_type=jnp.float32
     )
     rows_send[...] = total.astype(jnp.bfloat16).reshape(rows_send.shape)
     sent += dispatch(rows_send, rows_all, rows_sems, rows_wall_sems)
+    sent += pass_on(marks_all, marks_sems, marks_wall_sems)
     for b in range(2):
         new_ref.reshape(flat, 128)[pl.ds(b, POINTS, stride=2)] = new[:POINTS, b * 128 : (b + 1) * 128]
     sent += pass_on(rows_all, rows_sems, rows_wall_sems)
@@ -489,7 +493,6 @@
             pltpu.VMEM((2, FACES, 256), jnp.float32),
             pltpu.VMEM((2, FACES, 128), jnp.float32),
             pltpu.VMEM((2, FACES, 128), jnp.float32),
-            pltpu.VMEM((128, 256), jnp.float32),
             pltpu.VMEM((spans, CAP, features), jnp.bfloat16),
             pltpu.VMEM((spans, marks, wide), jnp.bfloat16),
             dma((9,)), dma((4,)), dma((4,)),

time: 21.8 us -> 19.9 us (0.913)
  Pallas kernels: 20.9 us -> 19 us
    pallas_call x1, Pallas kernels: 18.7 us -> 16.8 us  [local(): pl.pallas_call(functools.partial(section_kernel, spans, walls), out_shape...]
where the time goes in v6:
time: 19.9 us; the launch traced here: 19.8 us
  Pallas kernels  19 us (95%)
  between operations  0.72 us (4%)
    pallas_call x1, Pallas kernels, local(): pl.pallas_call(functools.partial(section_kernel, spans, walls), out_shape...  16.8 us
    pallas_call x1, Pallas kernels, local(): pl.pallas_call(functools.partial(train_kernel, per_chunk, full), out_shap...  2.21 us

profile of v6, /device:TPU:0, one launch (start us, length us, event | category | flops | bytes accessed | tf_op | source)
XLA Modules:
  0.0 19.8 jit_solution(3535724750349638550)
XLA Ops:
  0.6 0.0 copy-start
  0.6 0.0 copy-start.1
  0.7 0.0 copy-start.2
  0.7 0.0 copy-start.3
  0.7 0.0 copy-start.4
  0.7 16.8 %section.1 = (f32[5,5,5,2,128]{4,3,2,1,0:T(2,128)S(1)}, bf16[4,8,16,128]{3,2,1,0:T(8,128)(2,1)S(1)}, bf16[4,8,16,128]{3,2,1,0:T(8,128)(2,1)S(1)}) custom-call(f32[5,5,5,2,128]{4,3,2,1,0:T(2,128)} %bitcast.8, f32[3,5,5,5,2,128]{5,4,3,2,1,0:T(2,128)} %bitcast.7, s32[1,128]{1,0:T(1,128)} %bitcast.9, s32[1,128]{1,0:T(1,128)} %bitcast.10, ...), custom_call_target="tpu_custom_call" | custom-call | tf_op jit(solution)/shard_map/section/pallas_call | solution.py:473
  17.5 0.0 copy-done
  17.5 0.0 copy-done.1
  17.5 0.0 copy-done.2
  17.6 0.0 copy-done.3
  17.6 0.0 copy-done.4
  17.6 2.2 %train.1 = (f32[5,5,5,2,128]{4,3,2,1,0:T(2,128)}, f32[1,128,256]{2,1,0:T(8,128)}, f32[1,256,256]{2,1,0:T(8,128)}, f32[1,256,256]{2,1,0:T(8,128)}, f32[1,256,256]{2,1,0:T(8,128)}, /*index=5*/f32[1,256,128]{2,1,0:T(8,128)}) custom-call(f32[5,5,5,2,128]{4,3,2,1,0:T(2,128)S(1)} %get-tuple-element.15.new_ref, ...), custom_call_target="tpu_custom_call" | custom-call | tf_op jit(solution)/shard_map/train/pallas_call | solution.py:522
Async XLA Ops:
  0.6 16.9 %copy-start = (bf16[1,256,256]{2,1,0:T(8,128)(2,1)S(1)}, bf16[1,256,256]{2,1,0:T(8,128)(2,1)}, u32[]{:S(2)}) copy-start(bf16[1,256,256]{2,1,0:T(8,128)(2,1)} %two.1) | copy-start | bytes 393220
  0.6 16.9 %copy-start.1 = (bf16[1,256,256]{2,1,0:T(8,128)(2,1)S(1)}, bf16[1,256,256]{2,1,0:T(8,128)(2,1)}, u32[]{:S(2)}) copy-start(bf16[1,256,256]{2,1,0:T(8,128)(2,1)} %three.1) | copy-start | bytes 393220
  0.7 16.9 %copy-start.2 = (bf16[1,256,256]{2,1,0:T(8,128)(2,1)S(1)}, bf16[1,256,256]{2,1,0:T(8,128)(2,1)}, u32[]{:S(2)}) copy-start(bf16[1,256,256]{2,1,0:T(8,128)(2,1)} %four.1) | copy-start | bytes 393220
  0.7 16.9 %copy-start.3 = (bf16[1,128,256]{2,1,0:T(8,128)(2,1)S(1)}, bf16[1,128,256]{2,1,0:T(8,128)(2,1)}, u32[]{:S(2)}) copy-start(bf16[1,128,256]{2,1,0:T(8,128)(2,1)} %one.1) | copy-start | bytes 196612
  0.7 16.9 %copy-start.4 = (bf16[1,256,128]{2,1,0:T(8,128)(2,1)S(1)}, bf16[1,256,128]{2,1,0:T(8,128)(2,1)}, u32[]{:S(2)}) copy-start(bf16[1,256,128]{2,1,0:T(8,128)(2,1)} %five.1) | copy-start | bytes 196612
